TPU v7x, 512 devices: a whole 4x8x8 slice. The times are simulated.
512 devices in a mesh: dp: 32 (over z, x), seq: 16 (over y, core).
Axes of the slice: x: 4, y: 8, z: 8, core: 2. Of those that a mesh axis runs over, the one named last changes fastest.
Arguments:
- queries: bfloat16 [32, 16, 224, 1536], P('dp', 'seq')
- key_rows: bfloat16 [32, 16, 224, 1536], P('dp', 'seq')
- values: bfloat16 [32, 16, 224, 1536], P('dp', 'seq'), may hold values from -6 to 6
- cotangent: bfloat16 [32, 16, 224, 1536], P('dp', 'seq')
- frame_counts: int32 [32], replicated, may hold values from 2 to 16, as said below
- position_counts: int32 [32], replicated, may hold values from 56 to 224, as said below
- head_scale: float32 [12], replicated, may hold values from 0.5 to 2
- frame_slope: float32 [12], replicated, may hold values from 0.02 to 0.5
Outputs:
- grad_queries: bfloat16 [32, 16, 224, 1536], P('dp', 'seq')
- grad_keys: bfloat16 [32, 16, 224, 1536], P('dp', 'seq')
- grad_values: bfloat16 [32, 16, 224, 1536], P('dp', 'seq')
- grad_scale: float32 [12], replicated
- grad_slope: float32 [12], replicated
Inputs may be any that keep to these rules, and one draw needn't show every extreme that they name: `frame_counts`: frames in use of each clip, the others are padding; some clip uses all 16. `position_counts`: spatial tokens in use in each frame of a clip, the others are padding; some clip uses all 224.
All inputs are finite; a program needn't handle non-finite values.
Results may differ from a plain program's by a relative error of at most 0.0063.
Values may be sent and summed in bfloat16 or wider, within the bound.
No kernel may reach another device: no remote copies, remote signals or barrier semaphores. Data moves between devices by JAX's collectives and lax.ppermute only.
A program may use at most 64 MiB of HBM per device.

v0:
```python
import math

import jax
import jax.numpy as jnp
from jax import lax
from jax.sharding import PartitionSpec as P


def attend(queries, key_rows, values, grad_out, scale, coef, distance, key_live, token_form):
    key_form = token_form.replace("l", "m")
    head_size = queries.shape[-1]
    factor = scale / math.sqrt(head_size)
    raw_scores = jnp.einsum(
        token_form + "," + key_form + "->bhlm",
        queries,
        key_rows,
        preferred_element_type=jnp.float32,
    )
    scores = raw_scores * factor[:, None, None] - coef[:, None, None] * distance
    scores = jnp.where(key_live, scores, -jnp.inf)
    row_top = jnp.max(scores, axis=-1, keepdims=True)
    exponent = jnp.exp(scores - row_top)
    probability = exponent / jnp.sum(exponent, axis=-1, keepdims=True)
    weights = probability.astype(jnp.bfloat16)
    grad_probs = jnp.einsum(
        token_form + "," + key_form + "->bhlm", grad_out, values, preferred_element_type=jnp.float32
    )
    grad_values = jnp.einsum(
        "bhlm," + token_form + "->" + key_form,
        weights,
        grad_out,
        preferred_element_type=jnp.float32,
    )
    grad_scores = probability * (
        grad_probs - jnp.sum(probability * grad_probs, axis=-1, keepdims=True)
    )
    rounded = grad_scores.astype(jnp.bfloat16)
    grad_queries = (
        jnp.einsum(
            "bhlm," + key_form + "->" + token_form,
            rounded,
            key_rows,
            preferred_element_type=jnp.float32,
        )
        * factor[:, None]
    )
    grad_keys = (
        jnp.einsum(
            "bhlm," + token_form + "->" + key_form,
            rounded,
            queries,
            preferred_element_type=jnp.float32,
        )
        * factor[:, None]
    )
    scale_terms = jnp.sum(grad_scores * raw_scores, axis=(2, 3)) / math.sqrt(head_size)
    slope_terms = -jnp.sum(grad_scores * distance, axis=(2, 3))
    return (grad_queries, grad_keys, grad_values, scale_terms, slope_terms)


def local(
    queries, key_rows, values, cotangent, frame_counts, position_counts, head_scale, frame_slope
):
    local_frames = queries.shape[1]
    spatial = queries.shape[2]
    channels = queries.shape[3]
    heads = head_scale.shape[0]
    head_size = channels // heads
    groups = lax.axis_size("seq")
    frames_all = local_frames * groups
    clip_index = lax.axis_index("dp")
    seq_index = lax.axis_index("seq")
    frame_count = frame_counts[clip_index]
    position_count = position_counts[clip_index]
    shape_four = (local_frames, spatial, heads, head_size)
    query_four = queries.reshape(shape_four)
    key_four = key_rows.reshape(shape_four)
    value_four = values.reshape(shape_four)
    cot_four = cotangent.reshape(shape_four)
    frame_ids = seq_index * local_frames + jnp.arange(local_frames)
    frame_live = frame_ids < frame_count
    place_live = jnp.arange(spatial) < position_count
    live = frame_live[:, None] & place_live[None, :]
    masked = jnp.where(live[:, :, None, None], cot_four, jnp.zeros((), jnp.bfloat16))
    zero_heads = jnp.zeros((heads,), jnp.float32)
    flat_space = jnp.zeros((spatial, spatial), jnp.float32)
    frame_iota = jnp.arange(frames_all)
    steps_apart = jnp.abs(frame_iota[:, None] - frame_iota[None, :]).astype(jnp.float32)
    time_live = frame_iota < frame_count
    space_parts = (query_four, key_four, value_four, masked)
    space_grads = attend(
        space_parts[0],
        space_parts[1],
        space_parts[2],
        space_parts[3],
        head_scale,
        zero_heads,
        flat_space,
        place_live,
        "blhd",
    )
    moved = (
        lax.all_to_all(query_four, "seq", split_axis=1, concat_axis=0, tiled=True),
        lax.all_to_all(key_four, "seq", split_axis=1, concat_axis=0, tiled=True),
        lax.all_to_all(value_four, "seq", split_axis=1, concat_axis=0, tiled=True),
        lax.all_to_all(masked, "seq", split_axis=1, concat_axis=0, tiled=True),
    )
    time_grads = attend(
        moved[0],
        moved[1],
        moved[2],
        moved[3],
        head_scale,
        frame_slope,
        steps_apart,
        time_live,
        "lbhd",
    )
    returned = (
        lax.all_to_all(
            time_grads[0].astype(jnp.bfloat16), "seq", split_axis=0, concat_axis=1, tiled=True
        ),
        lax.all_to_all(
            time_grads[1].astype(jnp.bfloat16), "seq", split_axis=0, concat_axis=1, tiled=True
        ),
        lax.all_to_all(
            time_grads[2].astype(jnp.bfloat16), "seq", split_axis=0, concat_axis=1, tiled=True
        ),
    )
    back_grads = [returned[0], returned[1], returned[2]]
    time_scale = jnp.sum(time_grads[3], axis=0)
    time_slope = jnp.sum(time_grads[4], axis=0)
    scale_local = jnp.sum(space_grads[3], axis=0) + time_scale
    summed = lax.psum((scale_local, time_slope), ("dp", "seq"))
    outputs = []
    for index in range(3):
        total = space_grads[index] + back_grads[index].astype(jnp.float32)
        outputs.append(total.astype(jnp.bfloat16).reshape(1, local_frames, spatial, channels))
    return (outputs[0], outputs[1], outputs[2], summed[0], summed[1])


def solution(mesh):
    in_specs = (
        P("dp", "seq", None, None),
        P("dp", "seq", None, None),
        P("dp", "seq", None, None),
        P("dp", "seq", None, None),
        P(),
        P(),
        P(),
        P(),
    )
    out_specs = (
        P("dp", "seq", None, None),
        P("dp", "seq", None, None),
        P("dp", "seq", None, None),
        P(),
        P(),
    )
    return jax.shard_map(local, mesh=mesh, in_specs=in_specs, out_specs=out_specs, check_vma=False)
```

profile of v0, /device:TPU:1, one launch (start us, length us, event | category | flops | bytes accessed | tf_op | source)
XLA Modules:
  0.0 335.6 jit_solution(12499300168633732046)
XLA Ops:
  3.5 10.3 %all-to-all-start = ((bf16[1,224,12,128]{3,2,0,1:T(8,128)(2,1)}), bf16[1,224,12,128]{3,2,0,1:T(8,128)(2,1)S(1)}, u32[]{:S(2)}, u32[]{:S(2)}) async-start(bf16[1,224,12,128]{3,2,0,1:T(8,128)(2,1)} %copy.204), calls=%async_computation | async-start | bytes 1835008 | tf_op jit(solution)/shard_map/all_to_all | solution.py:103
  15.5 23.6 %all-to-all-done = bf16[1,224,12,128]{3,2,0,1:T(8,128)(2,1)S(1)} async-done(((bf16[1,224,12,128]{3,2,0,1:T(8,128)(2,1)}), bf16[1,224,12,128]{3,2,0,1:T(8,128)(2,1)S(1)}, u32[]{:S(2)}, u32[]{:S(2)}) %all-to-all-start) | async-done | bytes 688160 | tf_op jit(solution)/shard_map/all_to_all | solution.py:103
  39.1 3.5 %all-to-all-start.1 = ((bf16[1,224,12,128]{3,2,0,1:T(8,128)(2,1)}), bf16[1,224,12,128]{3,2,0,1:T(8,128)(2,1)S(1)}, u32[]{:S(2)}, u32[]{:S(2)}) async-start(bf16[1,224,12,128]{3,2,0,1:T(8,128)(2,1)} %copy.207), calls=%async_computation.1 | async-start | bytes 1835008 | tf_op jit(solution)/shard_map/all_to_all | solution.py:104
  49.1 18.7 %all-to-all-done.1 = bf16[1,224,12,128]{3,2,0,1:T(8,128)(2,1)S(1)} async-done(((bf16[1,224,12,128]{3,2,0,1:T(8,128)(2,1)}), bf16[1,224,12,128]{3,2,0,1:T(8,128)(2,1)S(1)}, u32[]{:S(2)}, u32[]{:S(2)}) %all-to-all-start.1) | async-done | bytes 688160 | tf_op jit(solution)/shard_map/all_to_all | solution.py:104
  67.7 4.2 %all-to-all-start.2 = ((bf16[1,224,12,128]{3,2,0,1:T(8,128)(2,1)}), bf16[1,224,12,128]{3,2,0,1:T(8,128)(2,1)}, u32[]{:S(2)}, u32[]{:S(2)}) async-start(bf16[1,224,12,128]{3,2,0,1:T(8,128)(2,1)} %copy.212), calls=%async_computation.2 | async-start | bytes 1835008 | tf_op jit(solution)/shard_map/all_to_all | solution.py:106
  73.7 22.8 %all-to-all-done.2 = bf16[1,224,12,128]{3,2,0,1:T(8,128)(2,1)} async-done(((bf16[1,224,12,128]{3,2,0,1:T(8,128)(2,1)}), bf16[1,224,12,128]{3,2,0,1:T(8,128)(2,1)}, u32[]{:S(2)}, u32[]{:S(2)}) %all-to-all-start.2) | async-done | bytes 688160 | tf_op jit(solution)/shard_map/all_to_all | solution.py:106
  96.5 4.2 %all-to-all-start.3 = ((bf16[1,224,12,128]{3,2,0,1:T(8,128)(2,1)}), bf16[1,224,12,128]{3,2,0,1:T(8,128)(2,1)}, u32[]{:S(2)}, u32[]{:S(2)}) async-start(bf16[1,224,12,128]{3,2,0,1:T(8,128)(2,1)} %copy.215), calls=%async_computation.3 | async-start | bytes 1835008 | tf_op jit(solution)/shard_map/all_to_all | solution.py:105
  103.8 21.5 %all-to-all-done.3 = bf16[1,224,12,128]{3,2,0,1:T(8,128)(2,1)} async-done(((bf16[1,224,12,128]{3,2,0,1:T(8,128)(2,1)}), bf16[1,224,12,128]{3,2,0,1:T(8,128)(2,1)}, u32[]{:S(2)}, u32[]{:S(2)}) %all-to-all-start.3) | async-done | bytes 688160 | tf_op jit(solution)/shard_map/all_to_all | solution.py:105
  125.3 2.3 multiply_reduce_fusion.4
  131.8 4.2 %all-to-all-start.5 = ((bf16[16,14,12,128]{3,1,2,0:T(8,128)(2,1)}), bf16[16,14,12,128]{3,1,2,0:T(8,128)(2,1)}, u32[]{:S(2)}, u32[]{:S(2)}) async-start(bf16[16,14,12,128]{3,1,2,0:T(8,128)(2,1)} %copy.227), calls=%async_computation.5 | async-start | bytes 1572864 | tf_op jit(solution)/shard_map/all_to_all | solution.py:123
  137.8 2.4 fusion.62
  143.3 14.7 %all-to-all-done.5 = bf16[16,14,12,128]{3,1,2,0:T(8,128)(2,1)} async-done(((bf16[16,14,12,128]{3,1,2,0:T(8,128)(2,1)}), bf16[16,14,12,128]{3,1,2,0:T(8,128)(2,1)}, u32[]{:S(2)}, u32[]{:S(2)}) %all-to-all-start.5) | async-done | bytes 688160 | tf_op jit(solution)/shard_map/all_to_all | solution.py:123
  158.0 4.4 %all-to-all-start.6 = ((bf16[16,14,12,128]{3,1,2,0:T(8,128)(2,1)}), bf16[16,14,12,128]{3,1,2,0:T(8,128)(2,1)}, u32[]{:S(2)}, u32[]{:S(2)}) async-start(bf16[16,14,12,128]{3,1,2,0:T(8,128)(2,1)} %copy.233), calls=%async_computation.6 | async-start | bytes 1572864 | tf_op jit(solution)/shard_map/all_to_all | solution.py:126
  162.3 3.1 multiply_reduce_fusion.1
  165.5 2.4 multiply_reduce_fusion
  170.3 13.6 %all-to-all-done.6 = bf16[16,14,12,128]{3,1,2,0:T(8,128)(2,1)} async-done(((bf16[16,14,12,128]{3,1,2,0:T(8,128)(2,1)}), bf16[16,14,12,128]{3,1,2,0:T(8,128)(2,1)}, u32[]{:S(2)}, u32[]{:S(2)}) %all-to-all-start.6) | async-done | bytes 688160 | tf_op jit(solution)/shard_map/all_to_all | solution.py:126
  183.9 4.2 %all-to-all-start.4 = ((bf16[16,14,12,128]{3,1,2,0:T(8,128)(2,1)}), bf16[16,14,12,128]{3,1,2,0:T(8,128)(2,1)}, u32[]{:S(2)}, u32[]{:S(2)}) async-start(bf16[16,14,12,128]{3,1,2,0:T(8,128)(2,1)} %copy.221), calls=%async_computation.4 | async-start | bytes 1572864 | tf_op jit(solution)/shard_map/all_to_all | solution.py:120
  190.5 109.9 %all-reduce = (f32[12]{0:T(128)}, f32[12]{0:T(128)}) all-reduce(f32[12]{0:T(128)} %multiply_add_fusion, f32[12]{0:T(128)} %neg.3), channel_id=1, replica_groups=mesh['dp'=32,'seq'=16] {'dp','seq'}, use_global_device_ids=true, to_apply=%region_9.10 | all-reduce | flops 24 | bytes 192 | tf_op jit(solution)/shard_map/psum | solution.py:134
  303.9 2.4 reshape.236
  306.3 3.4 %fusion.17 = bf16[1,224,12,128]{3,1,2,0:T(8,128)(2,1)} fusion(f32[1,224,12,128]{3,1,2,0:T(8,128)} %reshape.236, bf16[12,224,224]{1,2,0:T(8,128)(2,1)} %get-tuple-element.36, bf16[224,12,128]{0,2,1:T(8,128)(2,1)} %bitcast.87, f32[12]{0:T(128)} %copy-done.13), kind=kOutput, calls=%fused_computation.35 | convolution fusion | flops 155172864 | bytes 3956784 | tf_op jit(solution)/shard_map/bhlm,blhd->bmhd/dot_general | solution.py:48
  309.7 2.2 copy.230
  311.9 2.2 copy.238
  317.7 2.4 reshape.237
  320.1 3.6 %add_convert_fusion = bf16[1,224,12,128]{3,1,2,0:T(8,128)(2,1)} fusion(f32[1,224,12,128]{3,1,2,0:T(8,128)} %reshape.237, bf16[224,12,128]{0,2,1:T(8,128)(2,1)} %bitcast.90, pred[224]{0:T(512)(128)(4,1)} %copy-done.19, f32[12,224]{1,0:T(8,128)S(1)} %get-tuple-element.41, f32[12,224,224]{1,2,0:T(8,128)S(1)} %fusion.63, f32[12]{0:T(128)} %copy-done.13, ...), kind=kOutput, calls=%fused_computation.23 | convolution fusion | flops 158186336 | bytes 5172208 | tf_op jit(solution)/shard_map/bhlm,blhd->bmhd/dot_general | solution.py:28
  (97 shorter events, 47.7 us)
Async XLA Ops:
  2.0 11.7 %copy-start.11 = (bf16[1,1,224,1536]{3,2,1,0:T(8,128)(2,1)S(1)}, bf16[1,1,224,1536]{3,2,1,0:T(8,128)(2,1)}, u32[]{:S(2)}) copy-start(bf16[1,1,224,1536]{3,2,1,0:T(8,128)(2,1)} %param.9) | copy-start | bytes 2064388
  3.5 35.6 %all-to-all-start = ((bf16[1,224,12,128]{3,2,0,1:T(8,128)(2,1)}), bf16[1,224,12,128]{3,2,0,1:T(8,128)(2,1)S(1)}, u32[]{:S(2)}, u32[]{:S(2)}) async-start(bf16[1,224,12,128]{3,2,0,1:T(8,128)(2,1)} %copy.204), calls=%async_computation | async-start | bytes 1835008 | tf_op jit(solution)/shard_map/all_to_all | solution.py:103
  14.0 28.6 %copy-start.21 = (s32[32]{0:T(128)S(1)}, s32[32]{0:T(128)}, u32[]{:S(2)}) copy-start(s32[32]{0:T(128)} %param.12) | copy-start | bytes 388
  14.0 29.2 %copy-start.22 = (s32[32]{0:T(128)S(1)}, s32[32]{0:T(128)}, u32[]{:S(2)}) copy-start(s32[32]{0:T(128)} %param.13) | copy-start | bytes 388
  39.1 4.1 %copy-start.7 = (bf16[1,224,12,128]{3,2,0,1:T(8,128)(2,1)}, bf16[1,224,12,128]{3,2,0,1:T(8,128)(2,1)S(1)}, u32[]{:S(2)}) copy-start(bf16[1,224,12,128]{3,2,0,1:T(8,128)(2,1)S(1)} %all-to-all-done) | copy-start | bytes 2064388
  39.1 28.6 %all-to-all-start.1 = ((bf16[1,224,12,128]{3,2,0,1:T(8,128)(2,1)}), bf16[1,224,12,128]{3,2,0,1:T(8,128)(2,1)S(1)}, u32[]{:S(2)}, u32[]{:S(2)}) async-start(bf16[1,224,12,128]{3,2,0,1:T(8,128)(2,1)} %copy.207), calls=%async_computation.1 | async-start | bytes 1835008 | tf_op jit(solution)/shard_map/all_to_all | solution.py:104
  45.2 3.9 %copy-start.3 = (bf16[1,1,224,1536]{2,3,1,0:T(8,128)(2,1)}, bf16[1,1,224,1536]{2,3,1,0:T(8,128)(2,1)S(1)}, u32[]{:S(2)}) copy-start(bf16[1,1,224,1536]{2,3,1,0:T(8,128)(2,1)S(1)} %copy.197) | copy-start | bytes 2064388
  49.1 22.9 %copy-start.12 = (bf16[1,1,224,1536]{3,2,1,0:T(8,128)(2,1)S(1)}, bf16[1,1,224,1536]{3,2,1,0:T(8,128)(2,1)}, u32[]{:S(2)}) copy-start(bf16[1,1,224,1536]{3,2,1,0:T(8,128)(2,1)} %param.10) | copy-start | bytes 2064388
  67.7 59.8 %copy-start.5 = (bf16[1,224,12,128]{3,2,0,1:T(8,128)(2,1)}, bf16[1,224,12,128]{3,2,0,1:T(8,128)(2,1)S(1)}, u32[]{:S(2)}) copy-start(bf16[1,224,12,128]{3,2,0,1:T(8,128)(2,1)S(1)} %all-to-all-done.1) | copy-start | bytes 2064388
  67.7 28.8 %all-to-all-start.2 = ((bf16[1,224,12,128]{3,2,0,1:T(8,128)(2,1)}), bf16[1,224,12,128]{3,2,0,1:T(8,128)(2,1)}, u32[]{:S(2)}, u32[]{:S(2)}) async-start(bf16[1,224,12,128]{3,2,0,1:T(8,128)(2,1)} %copy.212), calls=%async_computation.2 | async-start | bytes 1835008 | tf_op jit(solution)/shard_map/all_to_all | solution.py:106
  72.2 24.3 %copy-start.4 = (bf16[1,1,224,1536]{2,3,1,0:T(8,128)(2,1)}, bf16[1,1,224,1536]{2,3,1,0:T(8,128)(2,1)S(1)}, u32[]{:S(2)}) copy-start(bf16[1,1,224,1536]{2,3,1,0:T(8,128)(2,1)S(1)} %copy.198) | copy-start | bytes 2064388
  72.3 29.1 %copy-start.23 = (f32[12]{0:T(128)S(1)}, f32[12]{0:T(128)}, u32[]{:S(2)}) copy-start(f32[12]{0:T(128)} %param.14) | copy-start | bytes 148
  72.3 29.2 %copy-start.20 = (f32[12]{0:T(128)S(1)}, f32[12]{0:T(128)}, u32[]{:S(2)}) copy-start(f32[12]{0:T(128)} %param.15) | copy-start | bytes 148
  96.5 28.8 %all-to-all-start.3 = ((bf16[1,224,12,128]{3,2,0,1:T(8,128)(2,1)}), bf16[1,224,12,128]{3,2,0,1:T(8,128)(2,1)}, u32[]{:S(2)}, u32[]{:S(2)}) async-start(bf16[1,224,12,128]{3,2,0,1:T(8,128)(2,1)} %copy.215), calls=%async_computation.3 | async-start | bytes 1835008 | tf_op jit(solution)/shard_map/all_to_all | solution.py:105
  101.4 28.2 %copy-start.13 = (f32[12]{0:T(128)}, f32[12]{0:T(128)S(1)}, u32[]{:S(2)}) copy-start(f32[12]{0:T(128)S(1)} %broadcast_multiply_fusion.1) | copy-start | bytes 148
  103.8 23.8 %copy-start.24 = (f32[14,12,16,16]{2,3,1,0:T(8,128)}, f32[14,12,16,16]{2,3,1,0:T(8,128)S(1)}, u32[]{:S(2)}) copy-start(f32[14,12,16,16]{2,3,1,0:T(8,128)S(1)} %get-tuple-element.38) | copy-start | bytes 516100
  103.8 23.8 %copy-start.26 = (f32[14,12,16]{2,1,0:T(8,128)}, f32[14,12,16]{2,1,0:T(8,128)S(1)}, u32[]{:S(2)}) copy-start(f32[14,12,16]{2,1,0:T(8,128)S(1)} %get-tuple-element.37) | copy-start | bytes 32260
  131.8 26.1 %all-to-all-start.5 = ((bf16[16,14,12,128]{3,1,2,0:T(8,128)(2,1)}), bf16[16,14,12,128]{3,1,2,0:T(8,128)(2,1)}, u32[]{:S(2)}, u32[]{:S(2)}) async-start(bf16[16,14,12,128]{3,1,2,0:T(8,128)(2,1)} %copy.227), calls=%async_computation.5 | async-start | bytes 1572864 | tf_op jit(solution)/shard_map/all_to_all | solution.py:123
  158.0 25.9 %all-to-all-start.6 = ((bf16[16,14,12,128]{3,1,2,0:T(8,128)(2,1)}), bf16[16,14,12,128]{3,1,2,0:T(8,128)(2,1)}, u32[]{:S(2)}, u32[]{:S(2)}) async-start(bf16[16,14,12,128]{3,1,2,0:T(8,128)(2,1)} %copy.233), calls=%async_computation.6 | async-start | bytes 1572864 | tf_op jit(solution)/shard_map/all_to_all | solution.py:126
  162.3 3.1 copy-start.2
  165.4 2.5 copy-start.6
  165.4 2.5 copy-start.10
  165.5 2.4 copy-start.15
  183.9 142.3 %all-to-all-start.4 = ((bf16[16,14,12,128]{3,1,2,0:T(8,128)(2,1)}), bf16[16,14,12,128]{3,1,2,0:T(8,128)(2,1)}, u32[]{:S(2)}, u32[]{:S(2)}) async-start(bf16[16,14,12,128]{3,1,2,0:T(8,128)(2,1)} %copy.221), calls=%async_computation.4 | async-start | bytes 1572864 | tf_op jit(solution)/shard_map/all_to_all | solution.py:120
  (11 other events, 18.9 us)
where the time goes:
time: 338 us; the launch traced here: 336 us
  waiting for transfers between devices  115 us (34%)
  blocking collectives  110 us (33%)
  local copies, waits for them, and re-layouts  37.3 us (11%)
  starting transfers between devices  35 us (10%)
  matrix products  22.5 us (7%)
  other arithmetic  14.3 us (4%)
    psum x1, blocking collectives, local(): summed = lax.psum((scale_local, time_slope), ('dp', 'seq'))  110 us
    all_to_all x1, waiting for transfers between devices, local(): lax.all_to_all(query_four, 'seq', split_axis=1, concat_axis=0, tiled=True)  23.6 us
    all_to_all x1, waiting for transfers between devices, local(): lax.all_to_all(masked, 'seq', split_axis=1, concat_axis=0, tiled=True)  22.8 us
    all_to_all x1, waiting for transfers between devices, local(): lax.all_to_all(value_four, 'seq', split_axis=1, concat_axis=0, tiled=True)  21.5 us
    all_to_all x1, waiting for transfers between devices, local(): lax.all_to_all(key_four, 'seq', split_axis=1, concat_axis=0, tiled=True)  18.7 us
    all_to_all x1, waiting for transfers between devices, local(): lax.all_to_all(time_grads[1].astype(jnp.bfloat16), 'seq', split_axis=0, c...  14.7 us
    all_to_all x1, waiting for transfers between devices, local(): lax.all_to_all(time_grads[2].astype(jnp.bfloat16), 'seq', split_axis=0, c...  13.6 us
    convert_element_type x6, local copies, waits for them, and re-layouts, local(): total = space_grads[index] + back_grads[index].astype(jnp.float32)  12.3 us
  transfers between devices with their start and end apart: 7, of which 6 were waited for; matrix products, arithmetic and copies ran while one was open for 16% of the time, Pallas kernels for 0%

commit v1 on v0

v1 whole, which is shorter than its diff:
```python
import functools
import math

import jax
import jax.numpy as jnp
from jax import lax
from jax.experimental import pallas as pl
from jax.experimental.pallas import tpu as pltpu
from jax.sharding import PartitionSpec as P

HEAD = 128
ROW_SPLIT = 4
HEAD_SPLIT = 4
STEP = 8
BATCH = 7
SCOPED = 32 * 2**20
STREAM = 60 * 2**20


def dot(a, b, dims):
    return lax.dot_general(a, b, (dims, ((), ())), preferred_element_type=jnp.float32)


AB_T = ((1,), (1,))
AB = ((1,), (0,))
A_TB = ((0,), (0,))


def live_rows(fc_ref, pc_ref, shape):
    clip = lax.axis_index("dp")
    positions = jnp.where(lax.axis_index("seq") < fc_ref[clip], pc_ref[clip], 0)
    return lax.broadcasted_iota(jnp.int32, shape, 0) < positions


def pack_kernel(
    fc_ref, pc_ref, q_hbm, k_hbm, v_hbm, g_hbm, out_hbm, held_ref, out_ref, in_sem, out_sem
):
    spatial = held_ref.shape[1]
    rows, half = spatial // ROW_SPLIT, spatial // 2
    heads = out_ref.shape[1]
    width = heads * HEAD
    targets = out_ref.shape[0] // 2

    def fetch(index, part):
        here = pl.ds(part * half, half)
        return pltpu.make_async_copy(
            (q_hbm, k_hbm, v_hbm, g_hbm)[index].at[here], held_ref.at[index, here], in_sem.at[part, index]
        )

    def send(part):
        here = pl.ds(part * targets, targets)
        return pltpu.make_async_copy(out_ref.at[here], out_hbm.at[here], out_sem.at[part])

    for part in range(2):
        for index in range(4):
            fetch(index, part).start()
    live = live_rows(fc_ref, pc_ref, (spatial, width))
    for part in range(2):
        for index in range(4):
            fetch(index, part).wait()
            for group in range(HEAD_SPLIT):
                value = held_ref[index, pl.ds(part * half, half), pl.ds(group * width, width)]
                if index == 3:
                    value = jnp.where(live[part * half : (part + 1) * half], value, 0)
                    value = value.astype(jnp.bfloat16)
                for step in range(ROW_SPLIT // 2):
                    target = (part * (ROW_SPLIT // 2) + step) * HEAD_SPLIT + group
                    for head in range(heads):
                        out_ref[target, head, pl.ds(index * rows, rows), :] = value[
                            step * rows : (step + 1) * rows, head * HEAD : (head + 1) * HEAD
                        ]
        send(part).start()
    for part in range(2):
        send(part).wait()


def pack(frame_counts, position_counts, arrays):
    spatial, channels = arrays[0].shape
    rows = spatial // ROW_SPLIT
    smem = pl.BlockSpec(memory_space=pltpu.SMEM)
    hbm = pl.BlockSpec(memory_space=pltpu.HBM)
    shape = (ROW_SPLIT * HEAD_SPLIT, channels // (HEAD * HEAD_SPLIT), 4 * rows, HEAD)
    return pl.pallas_call(
        pack_kernel,
        in_specs=[smem] * 2 + [hbm] * 4,
        out_specs=hbm,
        out_shape=jax.ShapeDtypeStruct(shape, jnp.bfloat16),
        scratch_shapes=[
            pltpu.VMEM((4, spatial, channels), jnp.bfloat16),
            pltpu.VMEM(shape, jnp.bfloat16),
            pltpu.SemaphoreType.DMA((2, 4)),
            pltpu.SemaphoreType.DMA((2,)),
        ],
        compiler_params=pltpu.CompilerParams(vmem_limit_bytes=STREAM),
        cost_estimate=pl.CostEstimate(
            flops=0, bytes_accessed=4 * 4 * spatial * channels, transcendentals=0
        ),
        name="pack",
    )(frame_counts, position_counts, *arrays)


def space_kernel(
    fc_ref, pc_ref, scale_ref, q_ref, k_ref, v_ref, g_ref, dq_ref, dk_ref, dv_ref, sum_ref
):
    head = pl.program_id(0)
    factor = scale_ref[head] * (1.0 / math.sqrt(HEAD))
    query, key, value = q_ref[...], k_ref[...], v_ref[...]
    grad = g_ref[...]
    grad = jnp.where(live_rows(fc_ref, pc_ref, grad.shape), grad, 0).astype(grad.dtype)
    raw = dot(key, query, AB_T)
    key_row = lax.broadcasted_iota(jnp.int32, raw.shape, 0)
    live = key_row < pc_ref[lax.axis_index("dp")]
    scores = jnp.where(live, raw * factor, -jnp.inf)
    exponent = jnp.exp(scores - jnp.max(scores, axis=0, keepdims=True))
    prob = exponent * (1.0 / jnp.sum(exponent, axis=0, keepdims=True))
    grad_prob = dot(value, grad, AB_T)
    weighted = prob * grad_prob
    grad_score = weighted - prob * jnp.sum(weighted, axis=0, keepdims=True)
    rounded = grad_score.astype(jnp.bfloat16)
    dq_ref[...] = dot(rounded, key, A_TB) * factor
    dk_ref[...] = dot(rounded, query, AB) * factor
    dv_ref[...] = dot(prob.astype(jnp.bfloat16), grad, AB)
    term = jnp.sum(grad_score * raw) * (1.0 / math.sqrt(HEAD))
    lane = lax.broadcasted_iota(jnp.int32, sum_ref.shape, 1)

    @pl.when(head == 0)
    def _():
        sum_ref[...] = jnp.zeros_like(sum_ref)

    sum_ref[...] += jnp.where(lane == head, term, 0.0)


def space(frame_counts, position_counts, head_scale, arrays):
    spatial, channels = arrays[0].shape
    heads = channels // HEAD
    smem = pl.BlockSpec(memory_space=pltpu.SMEM)
    block = pl.BlockSpec((spatial, HEAD), lambda i: (0, i))
    return pl.pallas_call(
        space_kernel,
        grid=(heads,),
        in_specs=[smem] * 3 + [block] * 4,
        out_specs=[block] * 3 + [pl.BlockSpec((1, HEAD), lambda i: (0, 0))],
        out_shape=[jax.ShapeDtypeStruct((spatial, channels), jnp.float32)] * 3
        + [jax.ShapeDtypeStruct((1, HEAD), jnp.float32)],
        compiler_params=pltpu.CompilerParams(vmem_limit_bytes=SCOPED),
        cost_estimate=pl.CostEstimate(
            flops=10 * heads * spatial * spatial * HEAD,
            bytes_accessed=20 * spatial * channels,
            transcendentals=heads * spatial * spatial,
        ),
        name="space",
    )(frame_counts, position_counts, head_scale, *arrays)


def time_kernel(
    fc_ref, scale_ref, slope_ref, space_sum_ref, moved_ref, out_hbm, sum_ref, out_ref, out_sem
):
    frames = moved_ref.shape[0]
    heads = moved_ref.shape[1]
    rows = moved_ref.shape[2] // 4
    size = frames * STEP
    steps = rows // STEP
    group = lax.rem(lax.axis_index("seq"), HEAD_SPLIT)
    frame_count = fc_ref[lax.axis_index("dp")]
    row = lax.broadcasted_iota(jnp.int32, (size, size), 0)
    col = lax.broadcasted_iota(jnp.int32, (size, size), 1)
    row_frame, col_frame = row // STEP, col // STEP
    distance = jnp.abs(row_frame - col_frame).astype(jnp.float32)
    live = (lax.rem(row, STEP) == lax.rem(col, STEP)) & (row_frame < frame_count)
    sums = space_sum_ref[...]
    lane = lax.broadcasted_iota(jnp.int32, sums.shape, 1)
    sending = []
    for head in range(heads):
        which = group * heads + head
        factor = scale_ref[which] * (1.0 / math.sqrt(HEAD))
        bias = jnp.where(live, -slope_ref[which] * distance, -jnp.inf)

        def load(index, step):
            part = moved_ref[:, head, pl.ds(index * rows + step * STEP, STEP), :]
            return part.astype(jnp.float32).reshape(size, HEAD).astype(jnp.bfloat16)

        def store(index, step, value):
            value = value.reshape(frames, STEP, HEAD).astype(jnp.bfloat16)
            out_ref[:, head, pl.ds(index * rows + step * STEP, STEP), :] = value

        scale_terms = jnp.zeros((size, size), jnp.float32)
        slope_terms = jnp.zeros((size, size), jnp.float32)
        for first in range(0, steps, BATCH):
            batch = range(first, min(first + BATCH, steps))
            parts = [[load(index, step) for index in range(4)] for step in batch]
            raws = [dot(key, query, AB_T) for query, key, _, _ in parts]
            grad_probs = [dot(value, grad, AB_T) for _, _, value, grad in parts]
            scores = [raw * factor + bias for raw in raws]
            exponents = [jnp.exp(x - jnp.max(x, axis=0, keepdims=True)) for x in scores]
            probs = [x * (1.0 / jnp.sum(x, axis=0, keepdims=True)) for x in exponents]
            weighted = [x * y for x, y in zip(probs, grad_probs)]
            grad_scores = [
                x - y * jnp.sum(x, axis=0, keepdims=True) for x, y in zip(weighted, probs)
            ]
            for x, raw in zip(grad_scores, raws):
                scale_terms += x * raw
                slope_terms += x
            for step, (query, key, _, grad), prob, x in zip(batch, parts, probs, grad_scores):
                rounded = x.astype(jnp.bfloat16)
                store(0, step, dot(rounded, key, A_TB) * factor)
                store(1, step, dot(rounded, query, AB) * factor)
                store(2, step, dot(prob.astype(jnp.bfloat16), grad, AB))
        sent = pltpu.make_async_copy(
            out_ref.at[:, head], out_hbm.at[:, head], out_sem.at[head]
        )
        sent.start()
        sending.append(sent)
        scale_sum = jnp.sum(scale_terms) * (1.0 / math.sqrt(HEAD))
        slope_sum = -jnp.sum(slope_terms * distance)
        sums = sums + jnp.where(lane == which, scale_sum, 0.0)
        sums = sums + jnp.where(lane == heads * HEAD_SPLIT + which, slope_sum, 0.0)
    sum_ref[...] = jnp.broadcast_to(sums[None], sum_ref.shape)
    for sent in sending:
        sent.wait()


def time(frame_counts, head_scale, frame_slope, space_sum, moved):
    frames, heads, height, _ = moved.shape
    rows = height // 4
    smem = pl.BlockSpec(memory_space=pltpu.SMEM)
    vmem = pl.BlockSpec(memory_space=pltpu.VMEM)
    return pl.pallas_call(
        time_kernel,
        in_specs=[smem] * 3 + [vmem] * 2,
        out_specs=[pl.BlockSpec(memory_space=pltpu.HBM), vmem],
        out_shape=[
            pltpu.HBM((frames, heads, 3 * rows, HEAD), jnp.bfloat16),
            jax.ShapeDtypeStruct((frames, 1, HEAD), jnp.float32),
        ],
        scratch_shapes=[
            pltpu.VMEM((frames, heads, 3 * rows, HEAD), jnp.bfloat16),
            pltpu.SemaphoreType.DMA((heads,)),
        ],
        compiler_params=pltpu.CompilerParams(vmem_limit_bytes=SCOPED),
        cost_estimate=pl.CostEstimate(
            flops=10 * heads * rows * frames * frames * STEP * HEAD,
            bytes_accessed=14 * frames * rows * heads * HEAD,
            transcendentals=heads * rows * frames * frames * STEP,
        ),
        name="time",
    )(frame_counts, head_scale, frame_slope, space_sum, moved)


def add_kernel(back_ref, q_ref, k_ref, v_ref, oq_ref, ok_ref, ov_ref):
    rows = q_ref.shape[0] // ROW_SPLIT
    for index, (ref, out) in enumerate(((q_ref, oq_ref), (k_ref, ok_ref), (v_ref, ov_ref))):
        for part in range(ROW_SPLIT):
            for head in range(back_ref.shape[2]):
                here = (pl.ds(part * rows, rows), pl.ds(head * HEAD, HEAD))
                moved = back_ref[part, 0, head, pl.ds(index * rows, rows), :].astype(jnp.float32)
                out[here] = (ref[here] + moved).astype(jnp.bfloat16)


def add(back, arrays):
    spatial, channels = arrays[0].shape
    width = channels // HEAD_SPLIT
    rows = spatial // ROW_SPLIT
    block = pl.BlockSpec((spatial, width), lambda i: (0, i))
    return pl.pallas_call(
        add_kernel,
        grid=(HEAD_SPLIT,),
        in_specs=[
            pl.BlockSpec((ROW_SPLIT, 1, width // HEAD, 3 * rows, HEAD), lambda i: (0, i, 0, 0, 0))
        ]
        + [block] * 3,
        out_specs=[block] * 3,
        out_shape=[jax.ShapeDtypeStruct((spatial, channels), jnp.bfloat16)] * 3,
        compiler_params=pltpu.CompilerParams(vmem_limit_bytes=SCOPED),
        cost_estimate=pl.CostEstimate(
            flops=3 * spatial * channels, bytes_accessed=24 * spatial * channels, transcendentals=0
        ),
        name="add",
    )(back, *arrays)


def local(
    queries, key_rows, values, cotangent, frame_counts, position_counts, head_scale, frame_slope
):
    spatial, channels = queries.shape[2:]
    heads = head_scale.shape[0]
    clips = lax.axis_size("dp")
    arrays = [x.reshape(spatial, channels) for x in (queries, key_rows, values, cotangent)]
    exchange = functools.partial(
        lax.all_to_all, axis_name="seq", split_axis=0, concat_axis=0, tiled=True
    )
    packed = pack(frame_counts, position_counts, arrays)
    moved = exchange(packed)
    *space_grads, space_sum = space(frame_counts, position_counts, head_scale, arrays)
    grads, sums = time(frame_counts, head_scale, frame_slope, space_sum, moved)
    back = exchange(grads)
    stride = 1
    while stride < clips:
        sums = sums + lax.ppermute(sums, "dp", [(i, i ^ stride) for i in range(clips)])
        stride *= 2
    sums, back = lax.optimization_barrier((sums, back))
    sums = jnp.sum(exchange(sums), axis=(0, 1))
    back = back.reshape((ROW_SPLIT, HEAD_SPLIT) + back.shape[1:])
    outputs = add(back, space_grads)
    full = queries.shape
    return tuple(x.reshape(full) for x in outputs) + (sums[:heads], sums[heads : 2 * heads])


def solution(mesh):
    split = P("dp", "seq", None, None)
    return jax.shard_map(
        local,
        mesh=mesh,
        in_specs=(split,) * 4 + (P(),) * 4,
        out_specs=(split,) * 3 + (P(),) * 2,
        check_vma=False,
    )
```

time: 338 us -> 148 us (0.44)
  blocking collectives: 110 us -> 0 us
  waiting for transfers between devices: 115 us -> 76.2 us
  local copies, waits for them, and re-layouts: 37.3 us -> 9.89 us
  matrix products: 22.5 us -> 0 us
  Pallas kernels: 0 us -> 18.9 us
  other arithmetic: 14.3 us -> 0.68 us
  starting transfers between devices: 35 us -> 41.1 us
    psum x1 -> x0, blocking collectives: 110 us -> none  [local(): summed = lax.psum((scale_local, time_slope), ('dp', 'seq'))]
    all_to_all x7 -> x3, waiting for transfers between devices: 115 us -> 65.6 us  [the longest x1 46.5 us: local(): moved = exchange(packed)]
    convert_element_type x12 -> x0, local copies, waits for them, and re-layouts: 21.4 us -> none  [the longest x6 12.3 us: local(): total = space_grads[index] + back_grads[index].astype(jnp.float32)]
    dot_general x10 -> x0, matrix products: 20.3 us -> none  [the longest x2 5.36 us: attend(): jnp.einsum(token_form + ',' + key_form + '->bhlm', grad_out, values, pref...]
    ppermute x0 -> x5, starting transfers between devices: none -> 20.1 us  [local(): lax.ppermute(sums, 'dp', [(i, i ^ stride) for i in range(clips)])]
    pallas_call x0 -> x4, Pallas kernels: none -> 18.9 us  [the longest x1 9.45 us: space(): pl.pallas_call(space_kernel, grid=(heads,), in_specs=[smem] * 3 + [block]...]
    all_to_all x7 -> x3, starting transfers between devices: 35 us -> 21 us  [the longest x1 10.5 us: local(): moved = exchange(packed)]
    ppermute x0 -> x5, waiting for transfers between devices: none -> 10.6 us  [local(): lax.ppermute(sums, 'dp', [(i, i ^ stride) for i in range(clips)])]
  transfers between devices with their start and end apart: 7 -> 8, of which waited for: 6 -> 8; matrix products, arithmetic and copies ran while one was open for 16% -> 0% of each run, Pallas kernels for 0% -> 8%
where the time goes in v1:
time: 148 us; the launch traced here: 147 us
  waiting for transfers between devices  76.2 us (51%)
  starting transfers between devices  41.1 us (28%)
  Pallas kernels  18.9 us (13%)
  local copies, waits for them, and re-layouts  9.89 us (7%)
    all_to_all x1, waiting for transfers between devices, local(): moved = exchange(packed)  46.5 us
    ppermute x5, starting transfers between devices, local(): lax.ppermute(sums, 'dp', [(i, i ^ stride) for i in range(clips)])  20.1 us
    all_to_all x1, waiting for transfers between devices, local(): back = exchange(grads)  17 us
    ppermute x5, waiting for transfers between devices, local(): lax.ppermute(sums, 'dp', [(i, i ^ stride) for i in range(clips)])  10.6 us
    all_to_all x1, starting transfers between devices, local(): moved = exchange(packed)  10.5 us
    pallas_call x1, Pallas kernels, space(): pl.pallas_call(space_kernel, grid=(heads,), in_specs=[smem] * 3 + [block]...  9.45 us
    unnamed x28, local copies, waits for them, and re-layouts  9.31 us
    all_to_all x1, starting transfers between devices, local(): back = exchange(grads)  5.52 us
  transfers between devices with their start and end apart: 8, of which 8 were waited for; matrix products, arithmetic and copies ran while one was open for 0% of the time, Pallas kernels for 8%

profile of v1, /device:TPU:1, one launch (start us, length us, event | category | flops | bytes accessed | tf_op | source)
XLA Modules:
  0.0 147.5 jit_solution(17837391841323429118)
XLA Ops:
  0.6 3.6 %pack.1 = bf16[16,3,224,128]{3,2,1,0:T(8,128)(2,1)} custom-call(s32[32]{0:T(128)} %fc_ref.5, s32[32]{0:T(128)} %pc_ref.3, bf16[224,1536]{1,0:T(8,128)(2,1)} %bitcast.9, bf16[224,1536]{1,0:T(8,128)(2,1)} %bitcast.11, bf16[224,1536]{1,0:T(8,128)(2,1)} %bitcast.13, bf16[224,1536]{1,0:T(8,128)(2,1)} %bitcast.15), custom_call_target="tpu_custom_call" | custom-call | bytes 5505024 | tf_op jit(solution)/shard_map/pack/pallas_call | solution.py:83
  4.3 10.5 %all-to-all-start = ((bf16[16,3,224,128]{3,2,1,0:T(8,128)(2,1)}), bf16[16,3,224,128]{3,2,1,0:T(8,128)(2,1)S(1)}, u32[]{:S(2)}, u32[]{:S(2)}) async-start(bf16[16,3,224,128]{3,2,1,0:T(8,128)(2,1)} %pack.1), calls=%async_computation | async-start | bytes 5505024 | tf_op jit(solution)/shard_map/all_to_all | solution.py:292
  16.0 1.1 copy-done.8
  18.2 9.5 %space.1 = (f32[224,1536]{1,0:T(8,128)S(1)}, f32[224,1536]{1,0:T(8,128)S(1)}, f32[224,1536]{1,0:T(8,128)S(1)}, f32[1,128]{1,0:T(1,128)S(1)}) custom-call(s32[32]{0:T(128)S(1)} %copy-done.10, s32[32]{0:T(128)S(1)} %copy-done.11, f32[12]{0:T(128)S(1)} %copy-done.12, bf16[224,1536]{1,0:T(8,128)(2,1)S(1)} %bitcast.10, bf16[224,1536]{1,0:T(8,128)(2,1)S(1)} %bitcast.12, ...), custom_call_target="tpu_custom_call" | custom-call | flops 770703360 | bytes 6881280 | tf_op jit(solution)/shard_map/space/pallas_call | solution.py:138
  28.8 1.1 copy-done.2
  29.9 1.1 copy-done.4
  31.0 46.5 %all-to-all-done.moved_ref = bf16[16,3,224,128]{3,2,1,0:T(8,128)(2,1)S(1)} async-done(((bf16[16,3,224,128]{3,2,1,0:T(8,128)(2,1)}), bf16[16,3,224,128]{3,2,1,0:T(8,128)(2,1)S(1)}, u32[]{:S(2)}, u32[]{:S(2)}) %all-to-all-start) | async-done | bytes 2752544 | tf_op jit(solution)/shard_map/all_to_all | solution.py:292
  77.5 3.5 %time.1 = (bf16[16,3,168,128]{3,2,1,0:T(8,128)(2,1)}, f32[16,1,128]{2,1,0:T(1,128)S(1)}) custom-call(s32[32]{0:T(128)S(1)} %copy-done.10, f32[12]{0:T(128)S(1)} %copy-done.12, f32[12]{0:T(128)S(1)} %copy-done.13, f32[1,128]{1,0:T(1,128)S(1)} %get-tuple-element.16.space_sum_ref, bf16[16,3,224,128]{3,2,1,0:T(8,128)(2,1)S(1)} %all-to-all-done.moved_ref), custom_call_target="tpu_custom_call" | custom-call | flops 440401920 | bytes 4816896 | tf_op jit(solution)/shard_map/time/pallas_call | solution.py:227
  81.1 5.5 %all-to-all-start.1 = ((bf16[16,3,168,128]{3,2,1,0:T(8,128)(2,1)}), bf16[16,3,168,128]{3,2,1,0:T(8,128)(2,1)S(1)}, u32[]{:S(2)}, u32[]{:S(2)}) async-start(bf16[16,3,168,128]{3,2,1,0:T(8,128)(2,1)} %get-tuple-element.18), calls=%async_computation.1 | async-start | bytes 4128768 | tf_op jit(solution)/shard_map/all_to_all | solution.py:295
  86.6 1.9 %collective-permute-start = (f32[16,1,128]{2,1,0:T(1,128)S(1)}, f32[16,1,128]{2,1,0:T(1,128)S(1)}, u32[]{:S(2)}, u32[]{:S(2)}) collective-permute-start(f32[16,1,128]{2,1,0:T(1,128)S(1)} %get-tuple-element.17), channel_id=1, source_target_pairs={{0,16},{16,0},{32,48},{48,32},{64,80},{80,64},{96,112},{112,96},{1... | collective-permute-start | bytes 24584 | tf_op jit(solution)/shard_map/ppermute | solution.py:298
  88.5 2.5 %collective-permute-done = f32[16,1,128]{2,1,0:T(1,128)S(1)} collective-permute-done((f32[16,1,128]{2,1,0:T(1,128)S(1)}, f32[16,1,128]{2,1,0:T(1,128)S(1)}, u32[]{:S(2)}, u32[]{:S(2)}) %collective-permute-start) | collective-permute-done | bytes 8224 | tf_op jit(solution)/shard_map/ppermute | solution.py:298
  91.0 2.9 %collective-permute-start.1 = (f32[16,1,128]{2,1,0:T(1,128)S(1)}, f32[16,1,128]{2,1,0:T(1,128)S(1)}, u32[]{:S(2)}, u32[]{:S(2)}) collective-permute-start(f32[16,1,128]{2,1,0:T(1,128)S(1)} %add.16), channel_id=1, source_target_pairs={{0,32},{16,48},{32,0},{48,16},{64,96},{80,112},{96,64},{112,80},{1... | collective-permute-start | bytes 24584 | tf_op jit(solution)/shard_map/ppermute | solution.py:298
  93.9 3.2 %collective-permute-done.1 = f32[16,1,128]{2,1,0:T(1,128)S(1)} collective-permute-done((f32[16,1,128]{2,1,0:T(1,128)S(1)}, f32[16,1,128]{2,1,0:T(1,128)S(1)}, u32[]{:S(2)}, u32[]{:S(2)}) %collective-permute-start.1) | collective-permute-done | bytes 8224 | tf_op jit(solution)/shard_map/ppermute | solution.py:298
  97.1 2.2 %collective-permute-start.2 = (f32[16,1,128]{2,1,0:T(1,128)S(1)}, f32[16,1,128]{2,1,0:T(1,128)S(1)}, u32[]{:S(2)}, u32[]{:S(2)}) collective-permute-start(f32[16,1,128]{2,1,0:T(1,128)S(1)} %add.17), channel_id=1, source_target_pairs={{0,64},{16,80},{32,96},{48,112},{64,0},{80,16},{96,32},{112,48},{1... | collective-permute-start | bytes 24584 | tf_op jit(solution)/shard_map/ppermute | solution.py:298
  99.3 2.5 %collective-permute-done.2 = f32[16,1,128]{2,1,0:T(1,128)S(1)} collective-permute-done((f32[16,1,128]{2,1,0:T(1,128)S(1)}, f32[16,1,128]{2,1,0:T(1,128)S(1)}, u32[]{:S(2)}, u32[]{:S(2)}) %collective-permute-start.2) | collective-permute-done | bytes 8224 | tf_op jit(solution)/shard_map/ppermute | solution.py:298
  101.8 4.7 %collective-permute-start.3 = (f32[16,1,128]{2,1,0:T(1,128)S(1)}, f32[16,1,128]{2,1,0:T(1,128)S(1)}, u32[]{:S(2)}, u32[]{:S(2)}) collective-permute-start(f32[16,1,128]{2,1,0:T(1,128)S(1)} %add.18), channel_id=1, source_target_pairs={{0,128},{16,144},{32,160},{48,176},{64,192},{80,208},{96,224},{112... | collective-permute-start | bytes 24584 | tf_op jit(solution)/shard_map/ppermute | solution.py:298
  106.4 1.3 collective-permute-done.3
  107.8 8.4 %collective-permute-start.4 = (f32[16,1,128]{2,1,0:T(1,128)S(1)}, f32[16,1,128]{2,1,0:T(1,128)S(1)}, u32[]{:S(2)}, u32[]{:S(2)}) collective-permute-start(f32[16,1,128]{2,1,0:T(1,128)S(1)} %add.19), channel_id=1, source_target_pairs={{0,256},{16,272},{32,288},{48,304},{64,320},{80,336},{96,352},{112... | collective-permute-start | bytes 24584 | tf_op jit(solution)/shard_map/ppermute | solution.py:298
  117.9 17.0 %all-to-all-done.1 = bf16[16,3,168,128]{3,2,1,0:T(8,128)(2,1)S(1)} async-done(((bf16[16,3,168,128]{3,2,1,0:T(8,128)(2,1)}), bf16[16,3,168,128]{3,2,1,0:T(8,128)(2,1)S(1)}, u32[]{:S(2)}, u32[]{:S(2)}) %all-to-all-start.1) | async-done | bytes 2064416 | tf_op jit(solution)/shard_map/all_to_all | solution.py:295
  134.9 5.0 %all-to-all-start.2 = ((f32[16,1,128]{2,1,0:T(1,128)}), f32[16,1,128]{2,1,0:T(1,128)S(1)}, u32[]{:S(2)}, u32[]{:S(2)}) async-start(f32[16,1,128]{2,1,0:T(1,128)} %add.20), calls=%async_computation.2 | async-start | bytes 16384 | tf_op jit(solution)/shard_map/all_to_all | solution.py:301
  139.8 1.3 copy-done.3
  141.2 1.3 copy-done.5
  142.5 2.2 %add.21 = (bf16[224,1536]{1,0:T(8,128)(2,1)}, bf16[224,1536]{1,0:T(8,128)(2,1)}, bf16[224,1536]{1,0:T(8,128)(2,1)}) custom-call(bf16[4,4,3,168,128]{4,3,2,1,0:T(8,128)(2,1)S(1)} %bitcast.8, f32[224,1536]{1,0:T(8,128)S(1)} %copy-done.1, f32[224,1536]{1,0:T(8,128)S(1)} %copy-done.3, f32[224,1536]{1,0:T(8,128)S(1)} %copy-done.5), custom_call_target="tpu_custom_call" | custom-call | flops 1032192 | bytes 8257536 | tf_op jit(solution)/shard_map/add/pallas_call | solution.py:264
  144.7 2.1 %all-to-all-done.2 = f32[16,1,128]{2,1,0:T(1,128)S(1)} async-done(((f32[16,1,128]{2,1,0:T(1,128)}), f32[16,1,128]{2,1,0:T(1,128)S(1)}, u32[]{:S(2)}, u32[]{:S(2)}) %all-to-all-start.2) | async-done | bytes 8224 | tf_op jit(solution)/shard_map/all_to_all | solution.py:301
  (31 shorter events, 5.6 us)
Async XLA Ops:
  4.3 10.6 %copy-start.6 = (bf16[1,1,224,1536]{3,2,1,0:T(8,128)(2,1)S(1)}, bf16[1,1,224,1536]{3,2,1,0:T(8,128)(2,1)}, u32[]{:S(2)}) copy-start(bf16[1,1,224,1536]{3,2,1,0:T(8,128)(2,1)} %param.8) | copy-start | bytes 2064388
  4.3 10.6 %copy-start.10 = (s32[32]{0:T(128)S(1)}, s32[32]{0:T(128)}, u32[]{:S(2)}) copy-start(s32[32]{0:T(128)} %fc_ref.5) | copy-start | bytes 388
  4.3 10.6 %copy-start.11 = (s32[32]{0:T(128)S(1)}, s32[32]{0:T(128)}, u32[]{:S(2)}) copy-start(s32[32]{0:T(128)} %pc_ref.3) | copy-start | bytes 388
  4.3 10.6 %copy-start.12 = (f32[12]{0:T(128)S(1)}, f32[12]{0:T(128)}, u32[]{:S(2)}) copy-start(f32[12]{0:T(128)} %scale_ref.3) | copy-start | bytes 148
  4.3 73.2 %all-to-all-start = ((bf16[16,3,224,128]{3,2,1,0:T(8,128)(2,1)}), bf16[16,3,224,128]{3,2,1,0:T(8,128)(2,1)S(1)}, u32[]{:S(2)}, u32[]{:S(2)}) async-start(bf16[16,3,224,128]{3,2,1,0:T(8,128)(2,1)} %pack.1), calls=%async_computation | async-start | bytes 5505024 | tf_op jit(solution)/shard_map/all_to_all | solution.py:292
  14.9 1.1 copy-start.7
  16.0 1.1 copy-start.8
  17.1 1.1 copy-start.9
  18.2 59.3 %copy-start.13 = (f32[12]{0:T(128)S(1)}, f32[12]{0:T(128)}, u32[]{:S(2)}) copy-start(f32[12]{0:T(128)} %slope_ref.1) | copy-start | bytes 148
  27.7 1.1 copy-start
  28.8 1.1 copy-start.2
  29.9 1.1 copy-start.4
  81.1 58.8 %copy-start.1 = (f32[224,1536]{1,0:T(8,128)S(1)}, f32[224,1536]{1,0:T(8,128)}, u32[]{:S(2)}) copy-start(f32[224,1536]{1,0:T(8,128)} %copy-done) | copy-start | bytes 4128772
  81.1 53.8 %all-to-all-start.1 = ((bf16[16,3,168,128]{3,2,1,0:T(8,128)(2,1)}), bf16[16,3,168,128]{3,2,1,0:T(8,128)(2,1)S(1)}, u32[]{:S(2)}, u32[]{:S(2)}) async-start(bf16[16,3,168,128]{3,2,1,0:T(8,128)(2,1)} %get-tuple-element.18), calls=%async_computation.1 | async-start | bytes 4128768 | tf_op jit(solution)/shard_map/all_to_all | solution.py:295
  86.6 4.4 %collective-permute-start = (f32[16,1,128]{2,1,0:T(1,128)S(1)}, f32[16,1,128]{2,1,0:T(1,128)S(1)}, u32[]{:S(2)}, u32[]{:S(2)}) collective-permute-start(f32[16,1,128]{2,1,0:T(1,128)S(1)} %get-tuple-element.17), channel_id=1, source_target_pairs={{0,16},{16,0},{32,48},{48,32},{64,80},{80,64},{96,112},{112,96},{1... | collective-permute-start | bytes 24584 | tf_op jit(solution)/shard_map/ppermute | solution.py:298
  91.0 6.0 %collective-permute-start.1 = (f32[16,1,128]{2,1,0:T(1,128)S(1)}, f32[16,1,128]{2,1,0:T(1,128)S(1)}, u32[]{:S(2)}, u32[]{:S(2)}) collective-permute-start(f32[16,1,128]{2,1,0:T(1,128)S(1)} %add.16), channel_id=1, source_target_pairs={{0,32},{16,48},{32,0},{48,16},{64,96},{80,112},{96,64},{112,80},{1... | collective-permute-start | bytes 24584 | tf_op jit(solution)/shard_map/ppermute | solution.py:298
  97.1 4.7 %collective-permute-start.2 = (f32[16,1,128]{2,1,0:T(1,128)S(1)}, f32[16,1,128]{2,1,0:T(1,128)S(1)}, u32[]{:S(2)}, u32[]{:S(2)}) collective-permute-start(f32[16,1,128]{2,1,0:T(1,128)S(1)} %add.17), channel_id=1, source_target_pairs={{0,64},{16,80},{32,96},{48,112},{64,0},{80,16},{96,32},{112,48},{1... | collective-permute-start | bytes 24584 | tf_op jit(solution)/shard_map/ppermute | solution.py:298
  101.8 6.0 %collective-permute-start.3 = (f32[16,1,128]{2,1,0:T(1,128)S(1)}, f32[16,1,128]{2,1,0:T(1,128)S(1)}, u32[]{:S(2)}, u32[]{:S(2)}) collective-permute-start(f32[16,1,128]{2,1,0:T(1,128)S(1)} %add.18), channel_id=1, source_target_pairs={{0,128},{16,144},{32,160},{48,176},{64,192},{80,208},{96,224},{112... | collective-permute-start | bytes 24584 | tf_op jit(solution)/shard_map/ppermute | solution.py:298
  107.8 9.5 %collective-permute-start.4 = (f32[16,1,128]{2,1,0:T(1,128)S(1)}, f32[16,1,128]{2,1,0:T(1,128)S(1)}, u32[]{:S(2)}, u32[]{:S(2)}) collective-permute-start(f32[16,1,128]{2,1,0:T(1,128)S(1)} %add.19), channel_id=1, source_target_pairs={{0,256},{16,272},{32,288},{48,304},{64,320},{80,336},{96,352},{112... | collective-permute-start | bytes 24584 | tf_op jit(solution)/shard_map/ppermute | solution.py:298
  134.9 12.0 %all-to-all-start.2 = ((f32[16,1,128]{2,1,0:T(1,128)}), f32[16,1,128]{2,1,0:T(1,128)S(1)}, u32[]{:S(2)}, u32[]{:S(2)}) async-start(f32[16,1,128]{2,1,0:T(1,128)} %add.20), calls=%async_computation.2 | async-start | bytes 16384 | tf_op jit(solution)/shard_map/all_to_all | solution.py:301
  139.8 1.3 copy-start.3
  141.2 1.3 copy-start.5

commit v2 on v1

--- a/solution.py
+++ b/solution.py
@@ -13,6 +13,7 @@
 HEAD_SPLIT = 4
 STEP = 8
 BATCH = 7
+SPACE_TYPE = jnp.float32
 SCOPED = 32 * 2**20
 STREAM = 60 * 2**20
 
@@ -20,6 +21,8 @@
 def dot(a, b, dims):
     return lax.dot_general(a, b, (dims, ((), ())), preferred_element_type=jnp.float32)
 
+
+DISTANCES = {4: ((2, 1), (0, -1)), 8: ((4, -3), (3, -2), (0, 2), (1, -1))}
 
 AB_T = ((1,), (1,))
 AB = ((1,), (0,))
@@ -33,63 +36,87 @@
 
 
 def pack_kernel(
-    fc_ref, pc_ref, q_hbm, k_hbm, v_hbm, g_hbm, out_hbm, held_ref, out_ref, in_sem, out_sem
+    fc_hbm,
+    pc_hbm,
+    q_hbm,
+    k_hbm,
+    v_hbm,
+    g_hbm,
+    out_hbm,
+    fc_ref,
+    pc_ref,
+    held_ref,
+    out_ref,
+    count_sem,
+    in_sem,
+    out_sem,
 ):
     spatial = held_ref.shape[1]
-    rows, half = spatial // ROW_SPLIT, spatial // 2
+    rows = spatial // ROW_SPLIT
     heads = out_ref.shape[1]
     width = heads * HEAD
-    targets = out_ref.shape[0] // 2
-
-    def fetch(index, part):
-        here = pl.ds(part * half, half)
+
+    def fetch(index, group):
+        here = pl.ds(group * width, width)
         return pltpu.make_async_copy(
-            (q_hbm, k_hbm, v_hbm, g_hbm)[index].at[here], held_ref.at[index, here], in_sem.at[part, index]
+            (q_hbm, k_hbm, v_hbm, g_hbm)[index].at[:, here],
+            held_ref.at[index, :, here],
+            in_sem.at[group, index],
         )
 
-    def send(part):
-        here = pl.ds(part * targets, targets)
-        return pltpu.make_async_copy(out_ref.at[here], out_hbm.at[here], out_sem.at[part])
-
-    for part in range(2):
+    def send(group):
+        here = pl.ds(group * ROW_SPLIT, ROW_SPLIT)
+        return pltpu.make_async_copy(out_ref.at[here], out_hbm.at[here], out_sem.at[group])
+
+    counts = (
+        pltpu.make_async_copy(fc_hbm, fc_ref, count_sem.at[0]),
+        pltpu.make_async_copy(pc_hbm, pc_ref, count_sem.at[1]),
+    )
+    for index in range(4):
+        fetch(index, 0).start()
+    for count in counts:
+        count.start()
+    for group in range(1, HEAD_SPLIT):
         for index in range(4):
-            fetch(index, part).start()
-    live = live_rows(fc_ref, pc_ref, (spatial, width))
-    for part in range(2):
+            fetch(index, group).start()
+    for group in range(HEAD_SPLIT):
         for index in range(4):
-            fetch(index, part).wait()
-            for group in range(HEAD_SPLIT):
-                value = held_ref[index, pl.ds(part * half, half), pl.ds(group * width, width)]
-                if index == 3:
-                    value = jnp.where(live[part * half : (part + 1) * half], value, 0)
-                    value = value.astype(jnp.bfloat16)
-                for step in range(ROW_SPLIT // 2):
-                    target = (part * (ROW_SPLIT // 2) + step) * HEAD_SPLIT + group
-                    for head in range(heads):
-                        out_ref[target, head, pl.ds(index * rows, rows), :] = value[
-                            step * rows : (step + 1) * rows, head * HEAD : (head + 1) * HEAD
-                        ]
-        send(part).start()
-    for part in range(2):
-        send(part).wait()
+            fetch(index, group).wait()
+            if group == 0 and index == 3:
+                for count in counts:
+                    count.wait()
+                live = live_rows(fc_ref, pc_ref, (spatial, width))
+            value = held_ref[index, :, pl.ds(group * width, width)]
+            if index == 3:
+                value = jnp.where(live, value, 0).astype(jnp.bfloat16)
+            for part in range(ROW_SPLIT):
+                for head in range(heads):
+                    out_ref[group * ROW_SPLIT + part, head, pl.ds(index * rows, rows), :] = value[
+                        part * rows : (part + 1) * rows, head * HEAD : (head + 1) * HEAD
+                    ]
+        send(group).start()
+    for group in range(HEAD_SPLIT):
+        send(group).wait()
 
 
 def pack(frame_counts, position_counts, arrays):
     spatial, channels = arrays[0].shape
     rows = spatial // ROW_SPLIT
-    smem = pl.BlockSpec(memory_space=pltpu.SMEM)
     hbm = pl.BlockSpec(memory_space=pltpu.HBM)
     shape = (ROW_SPLIT * HEAD_SPLIT, channels // (HEAD * HEAD_SPLIT), 4 * rows, HEAD)
     return pl.pallas_call(
         pack_kernel,
-        in_specs=[smem] * 2 + [hbm] * 4,
+        in_specs=[hbm] * 6,
         out_specs=hbm,
-        out_shape=jax.ShapeDtypeStruct(shape, jnp.bfloat16),
+        out_shape=pltpu.HBM(shape, jnp.bfloat16),
         scratch_shapes=[
+            pltpu.SMEM(frame_counts.shape, jnp.int32),
+            pltpu.SMEM(position_counts.shape, jnp.int32),
             pltpu.VMEM((4, spatial, channels), jnp.bfloat16),
             pltpu.VMEM(shape, jnp.bfloat16),
-            pltpu.SemaphoreType.DMA((2, 4)),
             pltpu.SemaphoreType.DMA((2,)),
+            pltpu.SemaphoreType.DMA((HEAD_SPLIT, 4)),
+            pltpu.SemaphoreType.DMA((HEAD_SPLIT,)),
         ],
         compiler_params=pltpu.CompilerParams(vmem_limit_bytes=STREAM),
         cost_estimate=pl.CostEstimate(
@@ -117,9 +144,9 @@
     weighted = prob * grad_prob
     grad_score = weighted - prob * jnp.sum(weighted, axis=0, keepdims=True)
     rounded = grad_score.astype(jnp.bfloat16)
-    dq_ref[...] = dot(rounded, key, A_TB) * factor
-    dk_ref[...] = dot(rounded, query, AB) * factor
-    dv_ref[...] = dot(prob.astype(jnp.bfloat16), grad, AB)
+    dq_ref[...] = (dot(rounded, key, A_TB) * factor).astype(dq_ref.dtype)
+    dk_ref[...] = (dot(rounded, query, AB) * factor).astype(dk_ref.dtype)
+    dv_ref[...] = dot(prob.astype(jnp.bfloat16), grad, AB).astype(dv_ref.dtype)
     term = jnp.sum(grad_score * raw) * (1.0 / math.sqrt(HEAD))
     lane = lax.broadcasted_iota(jnp.int32, sum_ref.shape, 1)
 
@@ -140,7 +167,7 @@
         grid=(heads,),
         in_specs=[smem] * 3 + [block] * 4,
         out_specs=[block] * 3 + [pl.BlockSpec((1, HEAD), lambda i: (0, 0))],
-        out_shape=[jax.ShapeDtypeStruct((spatial, channels), jnp.float32)] * 3
+        out_shape=[jax.ShapeDtypeStruct((spatial, channels), SPACE_TYPE)] * 3
         + [jax.ShapeDtypeStruct((1, HEAD), jnp.float32)],
         compiler_params=pltpu.CompilerParams(vmem_limit_bytes=SCOPED),
         cost_estimate=pl.CostEstimate(
@@ -160,7 +187,7 @@
     rows = moved_ref.shape[2] // 4
     size = frames * STEP
     steps = rows // STEP
-    group = lax.rem(lax.axis_index("seq"), HEAD_SPLIT)
+    group = lax.div(lax.axis_index("seq"), ROW_SPLIT)
     frame_count = fc_ref[lax.axis_index("dp")]
     row = lax.broadcasted_iota(jnp.int32, (size, size), 0)
     col = lax.broadcasted_iota(jnp.int32, (size, size), 1)
@@ -214,7 +241,7 @@
         slope_sum = -jnp.sum(slope_terms * distance)
         sums = sums + jnp.where(lane == which, scale_sum, 0.0)
         sums = sums + jnp.where(lane == heads * HEAD_SPLIT + which, slope_sum, 0.0)
-    sum_ref[...] = jnp.broadcast_to(sums[None], sum_ref.shape)
+    sum_ref[...] = sums
     for sent in sending:
         sent.wait()
 
@@ -230,7 +257,7 @@
         out_specs=[pl.BlockSpec(memory_space=pltpu.HBM), vmem],
         out_shape=[
             pltpu.HBM((frames, heads, 3 * rows, HEAD), jnp.bfloat16),
-            jax.ShapeDtypeStruct((frames, 1, HEAD), jnp.float32),
+            jax.ShapeDtypeStruct((1, HEAD), jnp.float32),
         ],
         scratch_shapes=[
             pltpu.VMEM((frames, heads, 3 * rows, HEAD), jnp.bfloat16),
@@ -246,36 +273,98 @@
     )(frame_counts, head_scale, frame_slope, space_sum, moved)
 
 
-def add_kernel(back_ref, q_ref, k_ref, v_ref, oq_ref, ok_ref, ov_ref):
-    rows = q_ref.shape[0] // ROW_SPLIT
-    for index, (ref, out) in enumerate(((q_ref, oq_ref), (k_ref, ok_ref), (v_ref, ov_ref))):
-        for part in range(ROW_SPLIT):
-            for head in range(back_ref.shape[2]):
-                here = (pl.ds(part * rows, rows), pl.ds(head * HEAD, HEAD))
-                moved = back_ref[part, 0, head, pl.ds(index * rows, rows), :].astype(jnp.float32)
-                out[here] = (ref[here] + moved).astype(jnp.bfloat16)
+def add_kernel(
+    back_ref, q_hbm, k_hbm, v_hbm, oq_hbm, ok_hbm, ov_hbm, held_ref, out_ref, in_sem, out_sem
+):
+    rows = held_ref.shape[1] // ROW_SPLIT
+    heads = back_ref.shape[2]
+    width = heads * HEAD
+
+    def fetch(index, group):
+        here = pl.ds(group * width, width)
+        return pltpu.make_async_copy(
+            (q_hbm, k_hbm, v_hbm)[index].at[:, here],
+            held_ref.at[index, :, here],
+            in_sem.at[group, index],
+        )
+
+    def send(index, group):
+        here = pl.ds(group * width, width)
+        return pltpu.make_async_copy(
+            out_ref.at[index, :, here],
+            (oq_hbm, ok_hbm, ov_hbm)[index].at[:, here],
+            out_sem.at[group, index],
+        )
+
+    blocks = [(index, group) for group in range(HEAD_SPLIT) for index in range(3)]
+    for block in blocks:
+        fetch(*block).start()
+    for index, group in blocks:
+        fetch(index, group).wait()
+        for head in range(heads):
+            columns = pl.ds(group * width + head * HEAD, HEAD)
+            moved = [
+                back_ref[group, part, head, pl.ds(index * rows, rows), :].astype(jnp.float32)
+                for part in range(ROW_SPLIT)
+            ]
+            total = held_ref[index, :, columns].astype(jnp.float32) + jnp.concatenate(moved, axis=0)
+            out_ref[index, :, columns] = total.astype(jnp.bfloat16)
+        send(index, group).start()
+    for block in blocks:
+        send(*block).wait()
 
 
 def add(back, arrays):
     spatial, channels = arrays[0].shape
-    width = channels // HEAD_SPLIT
-    rows = spatial // ROW_SPLIT
-    block = pl.BlockSpec((spatial, width), lambda i: (0, i))
+    hbm = pl.BlockSpec(memory_space=pltpu.HBM)
     return pl.pallas_call(
         add_kernel,
-        grid=(HEAD_SPLIT,),
-        in_specs=[
-            pl.BlockSpec((ROW_SPLIT, 1, width // HEAD, 3 * rows, HEAD), lambda i: (0, i, 0, 0, 0))
-        ]
-        + [block] * 3,
-        out_specs=[block] * 3,
-        out_shape=[jax.ShapeDtypeStruct((spatial, channels), jnp.bfloat16)] * 3,
+        in_specs=[pl.BlockSpec(memory_space=pltpu.VMEM)] + [hbm] * 3,
+        out_specs=[hbm] * 3,
+        out_shape=[pltpu.HBM((spatial, channels), jnp.bfloat16)] * 3,
+        scratch_shapes=[
+            pltpu.VMEM((3, spatial, channels), arrays[0].dtype),
+            pltpu.VMEM((3, spatial, channels), jnp.bfloat16),
+            pltpu.SemaphoreType.DMA((HEAD_SPLIT, 3)),
+            pltpu.SemaphoreType.DMA((HEAD_SPLIT, 3)),
+        ],
         compiler_params=pltpu.CompilerParams(vmem_limit_bytes=SCOPED),
         cost_estimate=pl.CostEstimate(
             flops=3 * spatial * channels, bytes_accessed=24 * spatial * channels, transcendentals=0
         ),
         name="add",
-    )(back, *arrays)
+    )(back, *[pltpu.with_memory_space_constraint(x, pltpu.HBM) for x in arrays])
+
+
+def core_sum(sums):
+    cores = [[2 * i, 2 * i + 1] for i in range(lax.axis_size("seq") // 2)]
+    both = lax.all_gather(sums, "seq", axis=0, tiled=True, axis_index_groups=cores)
+    return jnp.sum(both, axis=0, keepdims=True)
+
+
+def ring_parts(sums, axis, stride, size):
+    clips, places = lax.axis_size("dp"), lax.axis_size("seq")
+    own = jnp.where(lax.rem(lax.axis_index("seq"), 2) == 0, sums, 0.0)
+    if size > lax.axis_size(axis) // stride:
+        return [own]
+
+    def source(clip, place, distance):
+        index = place if axis == "seq" else clip
+        here = index // stride % size
+        index += ((here + distance) % size - here) * stride
+        return (clip, index) if axis == "seq" else (index, place)
+
+    def receive(first, second):
+        pairs = []
+        for clip in range(clips):
+            for place in range(places):
+                distance = (first, second)[place % 2]
+                if distance:
+                    from_clip, from_place = source(clip, place, distance)
+                    pairs.append((from_clip * places + from_place, clip * places + place))
+        return lax.ppermute(sums, ("dp", "seq"), pairs)
+
+    return [own] + [receive(first, second) for first, second in DISTANCES[size]]
 
 
 def local(
@@ -283,7 +372,6 @@
 ):
     spatial, channels = queries.shape[2:]
     heads = head_scale.shape[0]
-    clips = lax.axis_size("dp")
     arrays = [x.reshape(spatial, channels) for x in (queries, key_rows, values, cotangent)]
     exchange = functools.partial(
         lax.all_to_all, axis_name="seq", split_axis=0, concat_axis=0, tiled=True
@@ -293,14 +381,17 @@
     *space_grads, space_sum = space(frame_counts, position_counts, head_scale, arrays)
     grads, sums = time(frame_counts, head_scale, frame_slope, space_sum, moved)
     back = exchange(grads)
-    stride = 1
-    while stride < clips:
-        sums = sums + lax.ppermute(sums, "dp", [(i, i ^ stride) for i in range(clips)])
-        stride *= 2
-    sums, back = lax.optimization_barrier((sums, back))
-    sums = jnp.sum(exchange(sums), axis=(0, 1))
-    back = back.reshape((ROW_SPLIT, HEAD_SPLIT) + back.shape[1:])
+    sums = core_sum(sums)
+    sums = core_sum(sum(ring_parts(sums, "dp", 1, 4)))
+    clips = lax.axis_size("dp")
+    for stride in (4, 8, 16):
+        if stride < clips:
+            sums = sums + lax.ppermute(sums, "dp", [(i, i ^ stride) for i in range(clips)])
+    parts = ring_parts(sums, "seq", 2, 8)
+    back = back.reshape((HEAD_SPLIT, ROW_SPLIT) + back.shape[1:])
     outputs = add(back, space_grads)
+    outputs, parts = lax.optimization_barrier((outputs, parts))
+    sums = core_sum(sum(parts))[0]
     full = queries.shape
     return tuple(x.reshape(full) for x in outputs) + (sums[:heads], sums[heads : 2 * heads])
 

time: 148 us -> 142 us (0.959)
  waiting for transfers between devices: 76.2 us -> 52.9 us
  starting transfers between devices: 41.1 us -> 55.4 us
  blocking collectives: 0 us -> 5.28 us
  local copies, waits for them, and re-layouts: 9.89 us -> 7.24 us
    ppermute x0 -> x6, starting transfers between devices: none -> 21.2 us  [receive(): return lax.ppermute(sums, ('dp', 'seq'), pairs)]
    all_to_all x1, waiting for transfers between devices: 17 us -> 0.01 us  [local(): back = exchange(grads)]
    ppermute x5 -> x3, waiting for transfers between devices: 10.6 us -> 3.33 us  [local(): lax.ppermute(sums, 'dp', [(i, i ^ stride) for i in range(clips)])]
    all_gather x0 -> x3, blocking collectives: none -> 5.28 us  [core_sum(): lax.all_gather(sums, 'seq', axis=0, tiled=True, axis_index_groups=cores)]
    all_to_all x1 -> x0, starting transfers between devices: 4.96 us -> none  [local(): sums = jnp.sum(exchange(sums), axis=(0, 1))]
    ppermute x0 -> x6, waiting for transfers between devices: none -> 3.08 us  [receive(): return lax.ppermute(sums, ('dp', 'seq'), pairs)]
    unnamed x28 -> x22, local copies, waits for them, and re-layouts: 9.31 us -> 6.65 us
    all_to_all x1 -> x0, waiting for transfers between devices: 2.13 us -> none  [local(): sums = jnp.sum(exchange(sums), axis=(0, 1))]
  transfers between devices with their start and end apart: 8 -> 11, of which waited for: 8 -> 5; matrix products, arithmetic and copies ran while one was open for 0% -> 0% of each run, Pallas kernels for 8% -> 9%
where the time goes in v2:
time: 142 us; the launch traced here: 141 us
  starting transfers between devices  55.4 us (39%)
  waiting for transfers between devices  52.9 us (37%)
  Pallas kernels  19.4 us (14%)
  local copies, waits for them, and re-layouts  7.24 us (5%)
  blocking collectives  5.28 us (4%)
    all_to_all x1, waiting for transfers between devices, local(): moved = exchange(packed)  46.5 us
    ppermute x6, starting transfers between devices, receive(): return lax.ppermute(sums, ('dp', 'seq'), pairs)  21.2 us
    ppermute x3, starting transfers between devices, local(): lax.ppermute(sums, 'dp', [(i, i ^ stride) for i in range(clips)])  18.2 us
    all_to_all x1, starting transfers between devices, local(): moved = exchange(packed)  10.5 us
    pallas_call x1, Pallas kernels, space(): pl.pallas_call(space_kernel, grid=(heads,), in_specs=[smem] * 3 + [block]...  9.45 us
    unnamed x22, local copies, waits for them, and re-layouts  6.65 us
    all_to_all x1, starting transfers between devices, local(): back = exchange(grads)  5.39 us
    all_gather x3, blocking collectives, core_sum(): lax.all_gather(sums, 'seq', axis=0, tiled=True, axis_index_groups=cores)  5.28 us
  transfers between devices with their start and end apart: 11, of which 5 were waited for; matrix products, arithmetic and copies ran while one was open for 0% of the time, Pallas kernels for 9%

profile of v2, /device:TPU:1, one launch (start us, length us, event | category | flops | bytes accessed | tf_op | source)
XLA Modules:
  0.0 141.2 jit_solution(11705594942099102301)
XLA Ops:
  0.6 3.0 %pack.1 = bf16[16,3,224,128]{3,2,1,0:T(8,128)(2,1)} custom-call(s32[32]{0:T(128)} %fc_ref.3, s32[32]{0:T(128)} %pc_hbm.1, bf16[224,1536]{1,0:T(8,128)(2,1)} %bitcast.18, bf16[224,1536]{1,0:T(8,128)(2,1)} %bitcast.20, bf16[224,1536]{1,0:T(8,128)(2,1)} %bitcast.22, bf16[224,1536]{1,0:T(8,128)(2,1)} %bitcast.24), custom_call_target="tpu_custom_call" | custom-call | bytes 5505024 | tf_op jit(solution)/shard_map/pack/pallas_call | solution.py:107
  3.7 10.5 %all-to-all-start = ((bf16[16,3,224,128]{3,2,1,0:T(8,128)(2,1)}), bf16[16,3,224,128]{3,2,1,0:T(8,128)(2,1)S(1)}, u32[]{:S(2)}, u32[]{:S(2)}) async-start(bf16[16,3,224,128]{3,2,1,0:T(8,128)(2,1)} %pack.1), calls=%async_computation | async-start | bytes 5505024 | tf_op jit(solution)/shard_map/all_to_all | solution.py:380
  17.6 9.4 %space.1 = (f32[224,1536]{1,0:T(8,128)S(1)}, f32[224,1536]{1,0:T(8,128)S(1)}, f32[224,1536]{1,0:T(8,128)S(1)}, f32[1,128]{1,0:T(1,128)S(1)}) custom-call(s32[32]{0:T(128)S(1)} %copy-done.7, s32[32]{0:T(128)S(1)} %copy-done.8, f32[12]{0:T(128)S(1)} %copy-done.9, bf16[224,1536]{1,0:T(8,128)(2,1)S(1)} %bitcast.19, bf16[224,1536]{1,0:T(8,128)(2,1)S(1)} %bitcast.21, ...), custom_call_target="tpu_custom_call" | custom-call | flops 770703360 | bytes 6881280 | tf_op jit(solution)/shard_map/space/pallas_call | solution.py:165
  27.0 1.1 copy-done
  28.1 1.1 copy-done.1
  30.4 46.5 %all-to-all-done.moved_ref = bf16[16,3,224,128]{3,2,1,0:T(8,128)(2,1)S(1)} async-done(((bf16[16,3,224,128]{3,2,1,0:T(8,128)(2,1)}), bf16[16,3,224,128]{3,2,1,0:T(8,128)(2,1)S(1)}, u32[]{:S(2)}, u32[]{:S(2)}) %all-to-all-start) | async-done | bytes 2752544 | tf_op jit(solution)/shard_map/all_to_all | solution.py:380
  76.9 3.5 %time.1 = (bf16[16,3,168,128]{3,2,1,0:T(8,128)(2,1)}, f32[1,128]{1,0:T(1,128)S(1)}) custom-call(s32[32]{0:T(128)S(1)} %copy-done.7, f32[12]{0:T(128)S(1)} %copy-done.9, f32[12]{0:T(128)S(1)} %copy-done.10, f32[1,128]{1,0:T(1,128)S(1)} %get-tuple-element.22.space_sum_ref, bf16[16,3,224,128]{3,2,1,0:T(8,128)(2,1)S(1)} %all-to-all-done.moved_ref), custom_call_target="tpu_custom_call" | custom-call | flops 440401920 | bytes 4816896 | tf_op jit(solution)/shard_map/time/pallas_call | solution.py:254
  80.4 5.4 %all-to-all-start.1 = ((bf16[16,3,168,128]{3,2,1,0:T(8,128)(2,1)}), bf16[16,3,168,128]{3,2,1,0:T(8,128)(2,1)S(1)}, u32[]{:S(2)}, u32[]{:S(2)}) async-start(bf16[16,3,168,128]{3,2,1,0:T(8,128)(2,1)} %get-tuple-element.23), calls=%async_computation.1 | async-start | bytes 4128768 | tf_op jit(solution)/shard_map/all_to_all | solution.py:383
  85.8 1.8 %all-gather = f32[2,1,128]{2,1,0:T(1,128)S(1)} all-gather(f32[1,1,128]{2,1,0:T(1,128)S(1)} %bitcast.26), channel_id=1, replica_groups={{0,1},{2,3},{4,5},{6,7},{8,9},{10,11},{12,13},{14,15},{16,17},{18,19},{..., dimensions={0}, use_global_device_ids=true | all-gather | bytes 1536 | tf_op jit(solution)/shard_map/all_gather | solution.py:341
  87.6 2.6 %collective-permute-start = (f32[1,128]{1,0:T(1,128)S(1)}, f32[1,128]{1,0:T(1,128)S(1)}, u32[]{:S(2)}, u32[]{:S(2)}) collective-permute-start(f32[1,128]{1,0:T(1,128)S(1)} %bitcast.27), channel_id=1, source_target_pairs={{32,0},{17,1},{34,2},{19,3},{36,4},{21,5},{38,6},{23,7},{40,8},{25... | collective-permute-start | bytes 1544 | tf_op jit(solution)/shard_map/ppermute | solution.py:365
  90.2 2.7 %collective-permute-start.1 = (f32[1,128]{1,0:T(1,128)S(1)}, f32[1,128]{1,0:T(1,128)S(1)}, u32[]{:S(2)}, u32[]{:S(2)}) collective-permute-start(f32[1,128]{1,0:T(1,128)S(1)} %bitcast.28), channel_id=1, source_target_pairs={{49,1},{51,3},{53,5},{55,7},{57,9},{59,11},{61,13},{63,15},{1,17},... | collective-permute-start | bytes 1544 | tf_op jit(solution)/shard_map/ppermute | solution.py:365
  92.9 3.1 %collective-permute-done.1 = f32[1,128]{1,0:T(1,128)S(1)} collective-permute-done((f32[1,128]{1,0:T(1,128)S(1)}, f32[1,128]{1,0:T(1,128)S(1)}, u32[]{:S(2)}, u32[]{:S(2)}) %collective-permute-start.1) | collective-permute-done | bytes 544 | tf_op jit(solution)/shard_map/ppermute | solution.py:365
  96.0 1.8 %all-gather.1 = f32[2,1,128]{2,1,0:T(1,128)S(1)} all-gather(f32[1,1,128]{2,1,0:T(1,128)S(1)} %fusion.2), channel_id=1, replica_groups={{0,1},{2,3},{4,5},{6,7},{8,9},{10,11},{12,13},{14,15},{16,17},{18,19},{..., dimensions={0}, use_global_device_ids=true | all-gather | bytes 1536 | tf_op jit(solution)/shard_map/all_gather | solution.py:341
  97.7 4.0 %collective-permute-start.2 = (f32[1,128]{1,0:T(1,128)S(1)}, f32[1,128]{1,0:T(1,128)S(1)}, u32[]{:S(2)}, u32[]{:S(2)}) collective-permute-start(f32[1,128]{1,0:T(1,128)S(1)} %bitcast.29), channel_id=1, source_target_pairs={{0,64},{16,80},{32,96},{48,112},{64,0},{80,16},{96,32},{112,48},{1... | collective-permute-start | bytes 1544 | tf_op jit(solution)/shard_map/ppermute | solution.py:389
  101.7 1.2 collective-permute-done.2
  103.0 5.8 %collective-permute-start.3 = (f32[1,128]{1,0:T(1,128)S(1)}, f32[1,128]{1,0:T(1,128)S(1)}, u32[]{:S(2)}, u32[]{:S(2)}) collective-permute-start(f32[1,128]{1,0:T(1,128)S(1)} %bitcast_add_fusion), channel_id=1, source_target_pairs={{0,128},{16,144},{32,160},{48,176},{64,192},{80,208},{96,224},{112... | collective-permute-start | bytes 1544 | tf_op jit(solution)/shard_map/ppermute | solution.py:389
  108.8 1.2 collective-permute-done.3
  110.0 8.4 %collective-permute-start.4 = (f32[1,128]{1,0:T(1,128)S(1)}, f32[1,128]{1,0:T(1,128)S(1)}, u32[]{:S(2)}, u32[]{:S(2)}) collective-permute-start(f32[1,128]{1,0:T(1,128)S(1)} %add.31), channel_id=1, source_target_pairs={{0,256},{16,272},{32,288},{48,304},{64,320},{80,336},{96,352},{112... | collective-permute-start | bytes 1544 | tf_op jit(solution)/shard_map/ppermute | solution.py:389
  119.3 5.2 %collective-permute-start.7 = (f32[1,128]{1,0:T(1,128)S(1)}, f32[1,128]{1,0:T(1,128)S(1)}, u32[]{:S(2)}, u32[]{:S(2)}) collective-permute-start(f32[1,128]{1,0:T(1,128)S(1)} %get-tuple-element.40), channel_id=1, source_target_pairs={{5,1},{7,3},{9,5},{11,7},{13,9},{15,11},{1,13},{3,15},{21,17},{23,... | collective-permute-start | bytes 1544 | tf_op jit(solution)/shard_map/ppermute | solution.py:365
  124.5 1.9 %collective-permute-start.6 = (f32[1,128]{1,0:T(1,128)S(1)}, f32[1,128]{1,0:T(1,128)S(1)}, u32[]{:S(2)}, u32[]{:S(2)}) collective-permute-start(f32[1,128]{1,0:T(1,128)S(1)} %get-tuple-element.40), channel_id=1, source_target_pairs={{6,0},{13,1},{8,2},{15,3},{10,4},{1,5},{12,6},{3,7},{14,8},{5,9},{... | collective-permute-start | bytes 1544 | tf_op jit(solution)/shard_map/ppermute | solution.py:365
  126.4 5.2 %collective-permute-start.5 = (f32[1,128]{1,0:T(1,128)S(1)}, f32[1,128]{1,0:T(1,128)S(1)}, u32[]{:S(2)}, u32[]{:S(2)}) collective-permute-start(f32[1,128]{1,0:T(1,128)S(1)} %get-tuple-element.40), channel_id=1, source_target_pairs={{8,0},{11,1},{10,2},{13,3},{12,4},{15,5},{14,6},{1,7},{0,8},{3,9},... | collective-permute-start | bytes 1544 | tf_op jit(solution)/shard_map/ppermute | solution.py:365
  131.6 3.7 %collective-permute-start.8 = (f32[1,128]{1,0:T(1,128)S(1)}, f32[1,128]{1,0:T(1,128)S(1)}, u32[]{:S(2)}, u32[]{:S(2)}) collective-permute-start(f32[1,128]{1,0:T(1,128)S(1)} %get-tuple-element.40), channel_id=1, source_target_pairs={{2,0},{15,1},{4,2},{1,3},{6,4},{3,5},{8,6},{5,7},{10,8},{7,9},{12,... | collective-permute-start | bytes 1544 | tf_op jit(solution)/shard_map/ppermute | solution.py:365
  135.3 3.4 %add.51 = (bf16[224,1536]{1,0:T(8,128)(2,1)}, bf16[224,1536]{1,0:T(8,128)(2,1)}, bf16[224,1536]{1,0:T(8,128)(2,1)}) custom-call(bf16[4,4,3,168,128]{4,3,2,1,0:T(8,128)(2,1)S(1)} %bitcast.17, f32[224,1536]{1,0:T(8,128)} %copy-done, f32[224,1536]{1,0:T(8,128)} %copy-done.1, f32[224,1536]{1,0:T(8,128)} %copy-done.2), custom_call_target="tpu_custom_call" | custom-call | flops 1032192 | bytes 8257536 | tf_op jit(solution)/shard_map/add/pallas_call | solution.py:320
  138.8 1.8 %all-gather.2 = f32[2,1,128]{2,1,0:T(1,128)S(1)} all-gather(f32[1,1,128]{2,1,0:T(1,128)S(1)} %add_bitcast_fusion), channel_id=1, replica_groups={{0,1},{2,3},{4,5},{6,7},{8,9},{10,11},{12,13},{14,15},{16,17},{18,19},{..., dimensions={0}, use_global_device_ids=true | all-gather | bytes 1536 | tf_op jit(solution)/shard_map/all_gather | solution.py:341
  (36 shorter events, 6.0 us)
Async XLA Ops:
  3.6 10.6 %copy-start.3 = (bf16[1,1,224,1536]{3,2,1,0:T(8,128)(2,1)S(1)}, bf16[1,1,224,1536]{3,2,1,0:T(8,128)(2,1)}, u32[]{:S(2)}) copy-start(bf16[1,1,224,1536]{3,2,1,0:T(8,128)(2,1)} %param.8) | copy-start | bytes 2064388
  3.6 10.6 %copy-start.7 = (s32[32]{0:T(128)S(1)}, s32[32]{0:T(128)}, u32[]{:S(2)}) copy-start(s32[32]{0:T(128)} %fc_ref.3) | copy-start | bytes 388
  3.7 10.6 %copy-start.8 = (s32[32]{0:T(128)S(1)}, s32[32]{0:T(128)}, u32[]{:S(2)}) copy-start(s32[32]{0:T(128)} %pc_hbm.1) | copy-start | bytes 388
  3.7 10.6 %copy-start.9 = (f32[12]{0:T(128)S(1)}, f32[12]{0:T(128)}, u32[]{:S(2)}) copy-start(f32[12]{0:T(128)} %scale_ref.3) | copy-start | bytes 148
  3.7 73.2 %all-to-all-start = ((bf16[16,3,224,128]{3,2,1,0:T(8,128)(2,1)}), bf16[16,3,224,128]{3,2,1,0:T(8,128)(2,1)S(1)}, u32[]{:S(2)}, u32[]{:S(2)}) async-start(bf16[16,3,224,128]{3,2,1,0:T(8,128)(2,1)} %pack.1), calls=%async_computation | async-start | bytes 5505024 | tf_op jit(solution)/shard_map/all_to_all | solution.py:380
  14.3 1.1 copy-start.4
  15.4 1.1 copy-start.5
  16.5 1.1 copy-start.6
  17.6 59.3 %copy-start.10 = (f32[12]{0:T(128)S(1)}, f32[12]{0:T(128)}, u32[]{:S(2)}) copy-start(f32[12]{0:T(128)} %slope_ref.1) | copy-start | bytes 148
  27.0 1.1 copy-start
  28.1 1.1 copy-start.1
  29.3 1.1 copy-start.2
  80.4 54.9 %all-to-all-start.1 = ((bf16[16,3,168,128]{3,2,1,0:T(8,128)(2,1)}), bf16[16,3,168,128]{3,2,1,0:T(8,128)(2,1)S(1)}, u32[]{:S(2)}, u32[]{:S(2)}) async-start(bf16[16,3,168,128]{3,2,1,0:T(8,128)(2,1)} %get-tuple-element.23), calls=%async_computation.1 | async-start | bytes 4128768 | tf_op jit(solution)/shard_map/all_to_all | solution.py:383
  87.6 5.3 %collective-permute-start = (f32[1,128]{1,0:T(1,128)S(1)}, f32[1,128]{1,0:T(1,128)S(1)}, u32[]{:S(2)}, u32[]{:S(2)}) collective-permute-start(f32[1,128]{1,0:T(1,128)S(1)} %bitcast.27), channel_id=1, source_target_pairs={{32,0},{17,1},{34,2},{19,3},{36,4},{21,5},{38,6},{23,7},{40,8},{25... | collective-permute-start | bytes 1544 | tf_op jit(solution)/shard_map/ppermute | solution.py:365
  90.2 5.8 %collective-permute-start.1 = (f32[1,128]{1,0:T(1,128)S(1)}, f32[1,128]{1,0:T(1,128)S(1)}, u32[]{:S(2)}, u32[]{:S(2)}) collective-permute-start(f32[1,128]{1,0:T(1,128)S(1)} %bitcast.28), channel_id=1, source_target_pairs={{49,1},{51,3},{53,5},{55,7},{57,9},{59,11},{61,13},{63,15},{1,17},... | collective-permute-start | bytes 1544 | tf_op jit(solution)/shard_map/ppermute | solution.py:365
  97.7 5.2 %collective-permute-start.2 = (f32[1,128]{1,0:T(1,128)S(1)}, f32[1,128]{1,0:T(1,128)S(1)}, u32[]{:S(2)}, u32[]{:S(2)}) collective-permute-start(f32[1,128]{1,0:T(1,128)S(1)} %bitcast.29), channel_id=1, source_target_pairs={{0,64},{16,80},{32,96},{48,112},{64,0},{80,16},{96,32},{112,48},{1... | collective-permute-start | bytes 1544 | tf_op jit(solution)/shard_map/ppermute | solution.py:389
  103.0 7.0 %collective-permute-start.3 = (f32[1,128]{1,0:T(1,128)S(1)}, f32[1,128]{1,0:T(1,128)S(1)}, u32[]{:S(2)}, u32[]{:S(2)}) collective-permute-start(f32[1,128]{1,0:T(1,128)S(1)} %bitcast_add_fusion), channel_id=1, source_target_pairs={{0,128},{16,144},{32,160},{48,176},{64,192},{80,208},{96,224},{112... | collective-permute-start | bytes 1544 | tf_op jit(solution)/shard_map/ppermute | solution.py:389
  110.0 9.4 %collective-permute-start.4 = (f32[1,128]{1,0:T(1,128)S(1)}, f32[1,128]{1,0:T(1,128)S(1)}, u32[]{:S(2)}, u32[]{:S(2)}) collective-permute-start(f32[1,128]{1,0:T(1,128)S(1)} %add.31), channel_id=1, source_target_pairs={{0,256},{16,272},{32,288},{48,304},{64,320},{80,336},{96,352},{112... | collective-permute-start | bytes 1544 | tf_op jit(solution)/shard_map/ppermute | solution.py:389
  119.3 19.4 %collective-permute-start.7 = (f32[1,128]{1,0:T(1,128)S(1)}, f32[1,128]{1,0:T(1,128)S(1)}, u32[]{:S(2)}, u32[]{:S(2)}) collective-permute-start(f32[1,128]{1,0:T(1,128)S(1)} %get-tuple-element.40), channel_id=1, source_target_pairs={{5,1},{7,3},{9,5},{11,7},{13,9},{15,11},{1,13},{3,15},{21,17},{23,... | collective-permute-start | bytes 1544 | tf_op jit(solution)/shard_map/ppermute | solution.py:365
  124.5 14.2 %collective-permute-start.6 = (f32[1,128]{1,0:T(1,128)S(1)}, f32[1,128]{1,0:T(1,128)S(1)}, u32[]{:S(2)}, u32[]{:S(2)}) collective-permute-start(f32[1,128]{1,0:T(1,128)S(1)} %get-tuple-element.40), channel_id=1, source_target_pairs={{6,0},{13,1},{8,2},{15,3},{10,4},{1,5},{12,6},{3,7},{14,8},{5,9},{... | collective-permute-start | bytes 1544 | tf_op jit(solution)/shard_map/ppermute | solution.py:365
  126.4 12.3 %collective-permute-start.5 = (f32[1,128]{1,0:T(1,128)S(1)}, f32[1,128]{1,0:T(1,128)S(1)}, u32[]{:S(2)}, u32[]{:S(2)}) collective-permute-start(f32[1,128]{1,0:T(1,128)S(1)} %get-tuple-element.40), channel_id=1, source_target_pairs={{8,0},{11,1},{10,2},{13,3},{12,4},{15,5},{14,6},{1,7},{0,8},{3,9},... | collective-permute-start | bytes 1544 | tf_op jit(solution)/shard_map/ppermute | solution.py:365
  131.6 7.2 %collective-permute-start.8 = (f32[1,128]{1,0:T(1,128)S(1)}, f32[1,128]{1,0:T(1,128)S(1)}, u32[]{:S(2)}, u32[]{:S(2)}) collective-permute-start(f32[1,128]{1,0:T(1,128)S(1)} %get-tuple-element.40), channel_id=1, source_target_pairs={{2,0},{15,1},{4,2},{1,3},{6,4},{3,5},{8,6},{5,7},{10,8},{7,9},{12,... | collective-permute-start | bytes 1544 | tf_op jit(solution)/shard_map/ppermute | solution.py:365

commit v3 on v2

--- a/solution.py
+++ b/solution.py
@@ -13,7 +13,7 @@
 HEAD_SPLIT = 4
 STEP = 8
 BATCH = 7
-SPACE_TYPE = jnp.float32
+SPACE_TYPE = jnp.bfloat16
 SCOPED = 32 * 2**20
 STREAM = 60 * 2**20
 
@@ -144,9 +144,10 @@
     weighted = prob * grad_prob
     grad_score = weighted - prob * jnp.sum(weighted, axis=0, keepdims=True)
     rounded = grad_score.astype(jnp.bfloat16)
-    dq_ref[...] = (dot(rounded, key, A_TB) * factor).astype(dq_ref.dtype)
-    dk_ref[...] = (dot(rounded, query, AB) * factor).astype(dk_ref.dtype)
-    dv_ref[...] = dot(prob.astype(jnp.bfloat16), grad, AB).astype(dv_ref.dtype)
+    here = pl.ds(head * HEAD, HEAD)
+    dq_ref[:, here] = (dot(rounded, key, A_TB) * factor).astype(dq_ref.dtype)
+    dk_ref[:, here] = (dot(rounded, query, AB) * factor).astype(dk_ref.dtype)
+    dv_ref[:, here] = dot(prob.astype(jnp.bfloat16), grad, AB).astype(dv_ref.dtype)
     term = jnp.sum(grad_score * raw) * (1.0 / math.sqrt(HEAD))
     lane = lax.broadcasted_iota(jnp.int32, sum_ref.shape, 1)
 
@@ -161,13 +162,14 @@
     spatial, channels = arrays[0].shape
     heads = channels // HEAD
     smem = pl.BlockSpec(memory_space=pltpu.SMEM)
+    vmem = pl.BlockSpec(memory_space=pltpu.VMEM)
     block = pl.BlockSpec((spatial, HEAD), lambda i: (0, i))
     return pl.pallas_call(
         space_kernel,
         grid=(heads,),
         in_specs=[smem] * 3 + [block] * 4,
-        out_specs=[block] * 3 + [pl.BlockSpec((1, HEAD), lambda i: (0, 0))],
-        out_shape=[jax.ShapeDtypeStruct((spatial, channels), SPACE_TYPE)] * 3
+        out_specs=[vmem] * 3 + [pl.BlockSpec((1, HEAD), lambda i: (0, 0))],
+        out_shape=[pltpu.VMEM((spatial, channels), SPACE_TYPE)] * 3
         + [jax.ShapeDtypeStruct((1, HEAD), jnp.float32)],
         compiler_params=pltpu.CompilerParams(vmem_limit_bytes=SCOPED),
         cost_estimate=pl.CostEstimate(
@@ -180,27 +182,50 @@
 
 
 def time_kernel(
-    fc_ref, scale_ref, slope_ref, space_sum_ref, moved_ref, out_hbm, sum_ref, out_ref, out_sem
+    fc_hbm,
+    scale_hbm,
+    slope_hbm,
+    space_sum_hbm,
+    moved_ref,
+    out_hbm,
+    sum_ref,
+    fc_ref,
+    scale_ref,
+    slope_ref,
+    space_sum_ref,
+    out_ref,
+    small_sem,
+    out_sem,
 ):
+    smalls = [
+        pltpu.make_async_copy(source, target, small_sem.at[index])
+        for index, (source, target) in enumerate(
+            (
+                (fc_hbm, fc_ref),
+                (scale_hbm, scale_ref),
+                (slope_hbm, slope_ref),
+                (space_sum_hbm, space_sum_ref),
+            )
+        )
+    ]
+    for small in smalls:
+        small.start()
     frames = moved_ref.shape[0]
     heads = moved_ref.shape[1]
     rows = moved_ref.shape[2] // 4
     size = frames * STEP
     steps = rows // STEP
     group = lax.div(lax.axis_index("seq"), ROW_SPLIT)
-    frame_count = fc_ref[lax.axis_index("dp")]
     row = lax.broadcasted_iota(jnp.int32, (size, size), 0)
     col = lax.broadcasted_iota(jnp.int32, (size, size), 1)
     row_frame, col_frame = row // STEP, col // STEP
     distance = jnp.abs(row_frame - col_frame).astype(jnp.float32)
-    live = (lax.rem(row, STEP) == lax.rem(col, STEP)) & (row_frame < frame_count)
-    sums = space_sum_ref[...]
+    same = lax.rem(row, STEP) == lax.rem(col, STEP)
+    sums = jnp.zeros(sum_ref.shape, jnp.float32)
     lane = lax.broadcasted_iota(jnp.int32, sums.shape, 1)
     sending = []
     for head in range(heads):
         which = group * heads + head
-        factor = scale_ref[which] * (1.0 / math.sqrt(HEAD))
-        bias = jnp.where(live, -slope_ref[which] * distance, -jnp.inf)
 
         def load(index, step):
             part = moved_ref[:, head, pl.ds(index * rows + step * STEP, STEP), :]
@@ -217,6 +242,14 @@
             parts = [[load(index, step) for index in range(4)] for step in batch]
             raws = [dot(key, query, AB_T) for query, key, _, _ in parts]
             grad_probs = [dot(value, grad, AB_T) for _, _, value, grad in parts]
+            if first == 0:
+                if head == 0:
+                    for small in smalls:
+                        small.wait()
+                    live = same & (row_frame < fc_ref[lax.axis_index("dp")])
+                    sums = space_sum_ref[...]
+                factor = scale_ref[which] * (1.0 / math.sqrt(HEAD))
+                bias = jnp.where(live, -slope_ref[which] * distance, -jnp.inf)
             scores = [raw * factor + bias for raw in raws]
             exponents = [jnp.exp(x - jnp.max(x, axis=0, keepdims=True)) for x in scores]
             probs = [x * (1.0 / jnp.sum(x, axis=0, keepdims=True)) for x in exponents]
@@ -249,18 +282,23 @@
 def time(frame_counts, head_scale, frame_slope, space_sum, moved):
     frames, heads, height, _ = moved.shape
     rows = height // 4
-    smem = pl.BlockSpec(memory_space=pltpu.SMEM)
+    hbm = pl.BlockSpec(memory_space=pltpu.HBM)
     vmem = pl.BlockSpec(memory_space=pltpu.VMEM)
     return pl.pallas_call(
         time_kernel,
-        in_specs=[smem] * 3 + [vmem] * 2,
-        out_specs=[pl.BlockSpec(memory_space=pltpu.HBM), vmem],
+        in_specs=[hbm] * 4 + [vmem],
+        out_specs=[hbm, vmem],
         out_shape=[
             pltpu.HBM((frames, heads, 3 * rows, HEAD), jnp.bfloat16),
             jax.ShapeDtypeStruct((1, HEAD), jnp.float32),
         ],
         scratch_shapes=[
+            pltpu.SMEM(frame_counts.shape, jnp.int32),
+            pltpu.SMEM(head_scale.shape, jnp.float32),
+            pltpu.SMEM(frame_slope.shape, jnp.float32),
+            pltpu.VMEM(space_sum.shape, jnp.float32),
             pltpu.VMEM((frames, heads, 3 * rows, HEAD), jnp.bfloat16),
+            pltpu.SemaphoreType.DMA((4,)),
             pltpu.SemaphoreType.DMA((heads,)),
         ],
         compiler_params=pltpu.CompilerParams(vmem_limit_bytes=SCOPED),
@@ -274,19 +312,11 @@
 
 
 def add_kernel(
-    back_ref, q_hbm, k_hbm, v_hbm, oq_hbm, ok_hbm, ov_hbm, held_ref, out_ref, in_sem, out_sem
+    back_ref, dq_ref, dk_ref, dv_ref, oq_hbm, ok_hbm, ov_hbm, out_ref, out_sem
 ):
-    rows = held_ref.shape[1] // ROW_SPLIT
+    rows = dv_ref.shape[0] // ROW_SPLIT
     heads = back_ref.shape[2]
     width = heads * HEAD
-
-    def fetch(index, group):
-        here = pl.ds(group * width, width)
-        return pltpu.make_async_copy(
-            (q_hbm, k_hbm, v_hbm)[index].at[:, here],
-            held_ref.at[index, :, here],
-            in_sem.at[group, index],
-        )
 
     def send(index, group):
         here = pl.ds(group * width, width)
@@ -296,18 +326,16 @@
             out_sem.at[group, index],
         )
 
-    blocks = [(index, group) for group in range(HEAD_SPLIT) for index in range(3)]
-    for block in blocks:
-        fetch(*block).start()
+    blocks = [(index, group) for index in range(3) for group in range(HEAD_SPLIT)]
     for index, group in blocks:
-        fetch(index, group).wait()
         for head in range(heads):
             columns = pl.ds(group * width + head * HEAD, HEAD)
             moved = [
                 back_ref[group, part, head, pl.ds(index * rows, rows), :].astype(jnp.float32)
                 for part in range(ROW_SPLIT)
             ]
-            total = held_ref[index, :, columns].astype(jnp.float32) + jnp.concatenate(moved, axis=0)
+            here = (dq_ref, dk_ref, dv_ref)[index][:, columns]
+            total = here.astype(jnp.float32) + jnp.concatenate(moved, axis=0)
             out_ref[index, :, columns] = total.astype(jnp.bfloat16)
         send(index, group).start()
     for block in blocks:
@@ -319,21 +347,19 @@
     hbm = pl.BlockSpec(memory_space=pltpu.HBM)
     return pl.pallas_call(
         add_kernel,
-        in_specs=[pl.BlockSpec(memory_space=pltpu.VMEM)] + [hbm] * 3,
+        in_specs=[pl.BlockSpec(memory_space=pltpu.VMEM)] * 4,
         out_specs=[hbm] * 3,
         out_shape=[pltpu.HBM((spatial, channels), jnp.bfloat16)] * 3,
         scratch_shapes=[
-            pltpu.VMEM((3, spatial, channels), arrays[0].dtype),
             pltpu.VMEM((3, spatial, channels), jnp.bfloat16),
-            pltpu.SemaphoreType.DMA((HEAD_SPLIT, 3)),
             pltpu.SemaphoreType.DMA((HEAD_SPLIT, 3)),
         ],
         compiler_params=pltpu.CompilerParams(vmem_limit_bytes=SCOPED),
         cost_estimate=pl.CostEstimate(
-            flops=3 * spatial * channels, bytes_accessed=24 * spatial * channels, transcendentals=0
+            flops=3 * spatial * channels, bytes_accessed=18 * spatial * channels, transcendentals=0
         ),
         name="add",
-    )(back, *[pltpu.with_memory_space_constraint(x, pltpu.HBM) for x in arrays])
+    )(back, *arrays)
 
 
 def core_sum(sums):

time: 142 us -> 140 us (0.986)
  Pallas kernels: 19.4 us -> 16.8 us
    ppermute x3, starting transfers between devices: 18.2 us -> 15.7 us  [local(): lax.ppermute(sums, 'dp', [(i, i ^ stride) for i in range(clips)])]
    ppermute x6, waiting for transfers between devices: 3.08 us -> 0.7 us  [receive(): return lax.ppermute(sums, ('dp', 'seq'), pairs)]
    ppermute x6, starting transfers between devices: 21.2 us -> 23.3 us  [receive(): return lax.ppermute(sums, ('dp', 'seq'), pairs)]
    pallas_call x1, Pallas kernels: 3.42 us -> 1.44 us  [add(): pl.pallas_call(add_kernel, in_specs=[pl.BlockSpec(memory_space=pltpu.VMEM...]
    unnamed x22 -> x28, local copies, waits for them, and re-layouts: 6.65 us -> 6.97 us
  transfers between devices with their start and end apart: 11 -> 11, of which waited for: 5 -> 6; matrix products, arithmetic and copies ran while one was open for 0% -> 0% of each run, Pallas kernels for 9% -> 8%
where the time goes in v3:
time: 140 us; the launch traced here: 139 us
  starting transfers between devices  55 us (39%)
  waiting for transfers between devices  53.1 us (38%)
  Pallas kernels  16.8 us (12%)
  local copies, waits for them, and re-layouts  7.55 us (5%)
  blocking collectives  5.81 us (4%)
    all_to_all x1, waiting for transfers between devices, local(): moved = exchange(packed)  47.7 us
    ppermute x6, starting transfers between devices, receive(): return lax.ppermute(sums, ('dp', 'seq'), pairs)  23.3 us
    ppermute x3, starting transfers between devices, local(): lax.ppermute(sums, 'dp', [(i, i ^ stride) for i in range(clips)])  15.7 us
    all_to_all x1, starting transfers between devices, local(): moved = exchange(packed)  10.5 us
    pallas_call x1, Pallas kernels, space(): pl.pallas_call(space_kernel, grid=(heads,), in_specs=[smem] * 3 + [block]...  9.02 us
    unnamed x28, local copies, waits for them, and re-layouts  6.97 us
    all_gather x3, blocking collectives, core_sum(): lax.all_gather(sums, 'seq', axis=0, tiled=True, axis_index_groups=cores)  5.81 us
    all_to_all x1, starting transfers between devices, local(): back = exchange(grads)  5.52 us
  transfers between devices with their start and end apart: 11, of which 6 were waited for; matrix products, arithmetic and copies ran while one was open for 0% of the time, Pallas kernels for 8%

profile of v3, /device:TPU:1, one launch (start us, length us, event | category | flops | bytes accessed | tf_op | source)
XLA Modules:
  0.0 139.2 jit_solution(7746610234447852555)
XLA Ops:
  0.6 3.0 %pack.1 = bf16[16,3,224,128]{3,2,1,0:T(8,128)(2,1)} custom-call(s32[32]{0:T(128)} %fc_hbm.3, s32[32]{0:T(128)} %pc_hbm.1, bf16[224,1536]{1,0:T(8,128)(2,1)} %bitcast.18, bf16[224,1536]{1,0:T(8,128)(2,1)} %bitcast.20, bf16[224,1536]{1,0:T(8,128)(2,1)} %bitcast.22, bf16[224,1536]{1,0:T(8,128)(2,1)} %bitcast.24), custom_call_target="tpu_custom_call" | custom-call | bytes 5505024 | tf_op jit(solution)/shard_map/pack/pallas_call | solution.py:107
  3.7 10.5 %all-to-all-start = ((bf16[16,3,224,128]{3,2,1,0:T(8,128)(2,1)}), bf16[16,3,224,128]{3,2,1,0:T(8,128)(2,1)S(1)}, u32[]{:S(2)}, u32[]{:S(2)}) async-start(bf16[16,3,224,128]{3,2,1,0:T(8,128)(2,1)} %pack.1), calls=%async_computation | async-start | bytes 5505024 | tf_op jit(solution)/shard_map/all_to_all | solution.py:406
  15.4 1.1 copy-done.2
  16.5 1.1 copy-done.3
  17.6 9.0 %space.1 = (bf16[224,1536]{1,0:T(8,128)(2,1)S(1)}, bf16[224,1536]{1,0:T(8,128)(2,1)S(1)}, bf16[224,1536]{1,0:T(8,128)(2,1)S(1)}, f32[1,128]{1,0:T(1,128)S(1)}) custom-call(s32[32]{0:T(128)S(1)} %copy-done.10, s32[32]{0:T(128)S(1)} %copy-done.11, f32[12]{0:T(128)S(1)} %copy-done.12, bf16[224,1536]{1,0:T(8,128)(2,1)S(1)} %bitcast.19, ...), custom_call_target="tpu_custom_call" | custom-call | flops 770703360 | bytes 6881280 | tf_op jit(solution)/shard_map/space/pallas_call | solution.py:167
  29.1 47.7 %all-to-all-done.moved_ref = bf16[16,3,224,128]{3,2,1,0:T(8,128)(2,1)S(1)} async-done(((bf16[16,3,224,128]{3,2,1,0:T(8,128)(2,1)}), bf16[16,3,224,128]{3,2,1,0:T(8,128)(2,1)S(1)}, u32[]{:S(2)}, u32[]{:S(2)}) %all-to-all-start) | async-done | bytes 2752544 | tf_op jit(solution)/shard_map/all_to_all | solution.py:406
  76.9 3.3 %time.1 = (bf16[16,3,168,128]{3,2,1,0:T(8,128)(2,1)}, f32[1,128]{1,0:T(1,128)S(1)}) custom-call(s32[32]{0:T(128)S(1)} %copy-done.10, f32[12]{0:T(128)S(1)} %copy-done.12, f32[12]{0:T(128)S(1)} %copy-done.13, f32[1,128]{1,0:T(1,128)S(1)} %get-tuple-element.22.space_sum_hbm, bf16[16,3,224,128]{3,2,1,0:T(8,128)(2,1)S(1)} %all-to-all-done.moved_ref), custom_call_target="tpu_custom_call" | custom-call | flops 440401920 | bytes 4816896 | tf_op jit(solution)/shard_map/time/pallas_call | solution.py:287
  80.2 5.5 %all-to-all-start.1 = ((bf16[16,3,168,128]{3,2,1,0:T(8,128)(2,1)}), bf16[16,3,168,128]{3,2,1,0:T(8,128)(2,1)S(1)}, u32[]{:S(2)}, u32[]{:S(2)}) async-start(bf16[16,3,168,128]{3,2,1,0:T(8,128)(2,1)} %get-tuple-element.23), calls=%async_computation.1 | async-start | bytes 4128768 | tf_op jit(solution)/shard_map/all_to_all | solution.py:409
  85.7 1.8 %all-gather = f32[2,1,128]{2,1,0:T(1,128)S(1)} all-gather(f32[1,1,128]{2,1,0:T(1,128)S(1)} %bitcast.26), channel_id=1, replica_groups={{0,1},{2,3},{4,5},{6,7},{8,9},{10,11},{12,13},{14,15},{16,17},{18,19},{..., dimensions={0}, use_global_device_ids=true | all-gather | bytes 1536 | tf_op jit(solution)/shard_map/all_gather | solution.py:367
  87.5 1.9 %collective-permute-start.1 = (f32[1,128]{1,0:T(1,128)S(1)}, f32[1,128]{1,0:T(1,128)S(1)}, u32[]{:S(2)}, u32[]{:S(2)}) collective-permute-start(f32[1,128]{1,0:T(1,128)S(1)} %bitcast.27), channel_id=1, source_target_pairs={{49,1},{51,3},{53,5},{55,7},{57,9},{59,11},{61,13},{63,15},{1,17},... | collective-permute-start | bytes 1544 | tf_op jit(solution)/shard_map/ppermute | solution.py:391
  89.4 4.6 %collective-permute-start = (f32[1,128]{1,0:T(1,128)S(1)}, f32[1,128]{1,0:T(1,128)S(1)}, u32[]{:S(2)}, u32[]{:S(2)}) collective-permute-start(f32[1,128]{1,0:T(1,128)S(1)} %bitcast.28), channel_id=1, source_target_pairs={{32,0},{17,1},{34,2},{19,3},{36,4},{21,5},{38,6},{23,7},{40,8},{25... | collective-permute-start | bytes 1544 | tf_op jit(solution)/shard_map/ppermute | solution.py:391
  94.7 2.1 %all-gather.1 = f32[2,1,128]{2,1,0:T(1,128)S(1)} all-gather(f32[1,1,128]{2,1,0:T(1,128)S(1)} %fusion.2), channel_id=1, replica_groups={{0,1},{2,3},{4,5},{6,7},{8,9},{10,11},{12,13},{14,15},{16,17},{18,19},{..., dimensions={0}, use_global_device_ids=true | all-gather | bytes 1536 | tf_op jit(solution)/shard_map/all_gather | solution.py:367
  96.8 2.4 %collective-permute-start.2 = (f32[1,128]{1,0:T(1,128)S(1)}, f32[1,128]{1,0:T(1,128)S(1)}, u32[]{:S(2)}, u32[]{:S(2)}) collective-permute-start(f32[1,128]{1,0:T(1,128)S(1)} %bitcast.29), channel_id=1, source_target_pairs={{0,64},{16,80},{32,96},{48,112},{64,0},{80,16},{96,32},{112,48},{1... | collective-permute-start | bytes 1544 | tf_op jit(solution)/shard_map/ppermute | solution.py:415
  99.2 2.2 %collective-permute-done.2 = f32[1,128]{1,0:T(1,128)S(1)} collective-permute-done((f32[1,128]{1,0:T(1,128)S(1)}, f32[1,128]{1,0:T(1,128)S(1)}, u32[]{:S(2)}, u32[]{:S(2)}) %collective-permute-start.2) | collective-permute-done | bytes 544 | tf_op jit(solution)/shard_map/ppermute | solution.py:415
  101.3 4.8 %collective-permute-start.3 = (f32[1,128]{1,0:T(1,128)S(1)}, f32[1,128]{1,0:T(1,128)S(1)}, u32[]{:S(2)}, u32[]{:S(2)}) collective-permute-start(f32[1,128]{1,0:T(1,128)S(1)} %bitcast_add_fusion), channel_id=1, source_target_pairs={{0,128},{16,144},{32,160},{48,176},{64,192},{80,208},{96,224},{112... | collective-permute-start | bytes 1544 | tf_op jit(solution)/shard_map/ppermute | solution.py:415
  106.2 1.2 collective-permute-done.3
  107.4 8.4 %collective-permute-start.4 = (f32[1,128]{1,0:T(1,128)S(1)}, f32[1,128]{1,0:T(1,128)S(1)}, u32[]{:S(2)}, u32[]{:S(2)}) collective-permute-start(f32[1,128]{1,0:T(1,128)S(1)} %add.31), channel_id=1, source_target_pairs={{0,256},{16,272},{32,288},{48,304},{64,320},{80,336},{96,352},{112... | collective-permute-start | bytes 1544 | tf_op jit(solution)/shard_map/ppermute | solution.py:415
  116.8 5.1 %collective-permute-start.5 = (f32[1,128]{1,0:T(1,128)S(1)}, f32[1,128]{1,0:T(1,128)S(1)}, u32[]{:S(2)}, u32[]{:S(2)}) collective-permute-start(f32[1,128]{1,0:T(1,128)S(1)} %get-tuple-element.40), channel_id=1, source_target_pairs={{8,0},{11,1},{10,2},{13,3},{12,4},{15,5},{14,6},{1,7},{0,8},{3,9},... | collective-permute-start | bytes 1544 | tf_op jit(solution)/shard_map/ppermute | solution.py:391
  121.9 4.0 %collective-permute-start.6 = (f32[1,128]{1,0:T(1,128)S(1)}, f32[1,128]{1,0:T(1,128)S(1)}, u32[]{:S(2)}, u32[]{:S(2)}) collective-permute-start(f32[1,128]{1,0:T(1,128)S(1)} %get-tuple-element.40), channel_id=1, source_target_pairs={{6,0},{13,1},{8,2},{15,3},{10,4},{1,5},{12,6},{3,7},{14,8},{5,9},{... | collective-permute-start | bytes 1544 | tf_op jit(solution)/shard_map/ppermute | solution.py:391
  125.9 3.4 %collective-permute-start.7 = (f32[1,128]{1,0:T(1,128)S(1)}, f32[1,128]{1,0:T(1,128)S(1)}, u32[]{:S(2)}, u32[]{:S(2)}) collective-permute-start(f32[1,128]{1,0:T(1,128)S(1)} %get-tuple-element.40), channel_id=1, source_target_pairs={{5,1},{7,3},{9,5},{11,7},{13,9},{15,11},{1,13},{3,15},{21,17},{23,... | collective-permute-start | bytes 1544 | tf_op jit(solution)/shard_map/ppermute | solution.py:391
  129.3 4.3 %collective-permute-start.8 = (f32[1,128]{1,0:T(1,128)S(1)}, f32[1,128]{1,0:T(1,128)S(1)}, u32[]{:S(2)}, u32[]{:S(2)}) collective-permute-start(f32[1,128]{1,0:T(1,128)S(1)} %get-tuple-element.40), channel_id=1, source_target_pairs={{2,0},{15,1},{4,2},{1,3},{6,4},{3,5},{8,6},{5,7},{10,8},{7,9},{12,... | collective-permute-start | bytes 1544 | tf_op jit(solution)/shard_map/ppermute | solution.py:391
  134.0 1.1 copy-done.9
  135.1 1.4 %add.51 = (bf16[224,1536]{1,0:T(8,128)(2,1)}, bf16[224,1536]{1,0:T(8,128)(2,1)}, bf16[224,1536]{1,0:T(8,128)(2,1)}) custom-call(bf16[4,4,3,168,128]{4,3,2,1,0:T(8,128)(2,1)S(1)} %bitcast.17, bf16[224,1536]{1,0:T(8,128)(2,1)S(1)} %copy-done.5, bf16[224,1536]{1,0:T(8,128)(2,1)S(1)} %copy-done.7, bf16[224,1536]{1,0:T(8,128)(2,1)S(1)} %copy-done.9), custom_call_target="tpu_custom_call" | custom-call | flops 1032192 | bytes 6193152 | tf_op jit(solution)/shard_map/add/pallas_call | solution.py:348
  136.6 2.0 %all-gather.2 = f32[2,1,128]{2,1,0:T(1,128)S(1)} all-gather(f32[1,1,128]{2,1,0:T(1,128)S(1)} %add_bitcast_fusion), channel_id=1, replica_groups={{0,1},{2,3},{4,5},{6,7},{8,9},{10,11},{12,13},{14,15},{16,17},{18,19},{..., dimensions={0}, use_global_device_ids=true | all-gather | bytes 1536 | tf_op jit(solution)/shard_map/all_gather | solution.py:367
  (42 shorter events, 6.3 us)
Async XLA Ops:
  3.6 10.6 %copy-start = (bf16[1,1,224,1536]{3,2,1,0:T(8,128)(2,1)S(1)}, bf16[1,1,224,1536]{3,2,1,0:T(8,128)(2,1)}, u32[]{:S(2)}) copy-start(bf16[1,1,224,1536]{3,2,1,0:T(8,128)(2,1)} %param.8) | copy-start | bytes 2064388
  3.6 10.6 %copy-start.10 = (s32[32]{0:T(128)S(1)}, s32[32]{0:T(128)}, u32[]{:S(2)}) copy-start(s32[32]{0:T(128)} %fc_hbm.3) | copy-start | bytes 388
  3.7 10.6 %copy-start.11 = (s32[32]{0:T(128)S(1)}, s32[32]{0:T(128)}, u32[]{:S(2)}) copy-start(s32[32]{0:T(128)} %pc_hbm.1) | copy-start | bytes 388
  3.7 10.6 %copy-start.12 = (f32[12]{0:T(128)S(1)}, f32[12]{0:T(128)}, u32[]{:S(2)}) copy-start(f32[12]{0:T(128)} %scale_hbm.1) | copy-start | bytes 148
  3.7 73.2 %all-to-all-start = ((bf16[16,3,224,128]{3,2,1,0:T(8,128)(2,1)}), bf16[16,3,224,128]{3,2,1,0:T(8,128)(2,1)S(1)}, u32[]{:S(2)}, u32[]{:S(2)}) async-start(bf16[16,3,224,128]{3,2,1,0:T(8,128)(2,1)} %pack.1), calls=%async_computation | async-start | bytes 5505024 | tf_op jit(solution)/shard_map/all_to_all | solution.py:406
  14.3 1.1 copy-start.1
  15.4 1.1 copy-start.2
  16.5 1.1 copy-start.3
  17.6 59.3 %copy-start.13 = (f32[12]{0:T(128)S(1)}, f32[12]{0:T(128)}, u32[]{:S(2)}) copy-start(f32[12]{0:T(128)} %slope_hbm.1) | copy-start | bytes 148
  26.6 0.8 copy-start.4
  27.4 0.8 copy-start.6
  80.2 53.8 %copy-start.5 = (bf16[224,1536]{1,0:T(8,128)(2,1)S(1)}, bf16[224,1536]{1,0:T(8,128)(2,1)}, u32[]{:S(2)}) copy-start(bf16[224,1536]{1,0:T(8,128)(2,1)} %copy-done.4) | copy-start | bytes 2064388
  80.2 53.8 %copy-start.7 = (bf16[224,1536]{1,0:T(8,128)(2,1)S(1)}, bf16[224,1536]{1,0:T(8,128)(2,1)}, u32[]{:S(2)}) copy-start(bf16[224,1536]{1,0:T(8,128)(2,1)} %copy-done.6) | copy-start | bytes 2064388
  80.2 53.8 %all-to-all-start.1 = ((bf16[16,3,168,128]{3,2,1,0:T(8,128)(2,1)}), bf16[16,3,168,128]{3,2,1,0:T(8,128)(2,1)S(1)}, u32[]{:S(2)}, u32[]{:S(2)}) async-start(bf16[16,3,168,128]{3,2,1,0:T(8,128)(2,1)} %get-tuple-element.23), calls=%async_computation.1 | async-start | bytes 4128768 | tf_op jit(solution)/shard_map/all_to_all | solution.py:409
  87.5 6.5 %collective-permute-start.1 = (f32[1,128]{1,0:T(1,128)S(1)}, f32[1,128]{1,0:T(1,128)S(1)}, u32[]{:S(2)}, u32[]{:S(2)}) collective-permute-start(f32[1,128]{1,0:T(1,128)S(1)} %bitcast.27), channel_id=1, source_target_pairs={{49,1},{51,3},{53,5},{55,7},{57,9},{59,11},{61,13},{63,15},{1,17},... | collective-permute-start | bytes 1544 | tf_op jit(solution)/shard_map/ppermute | solution.py:391
  89.4 5.3 %collective-permute-start = (f32[1,128]{1,0:T(1,128)S(1)}, f32[1,128]{1,0:T(1,128)S(1)}, u32[]{:S(2)}, u32[]{:S(2)}) collective-permute-start(f32[1,128]{1,0:T(1,128)S(1)} %bitcast.28), channel_id=1, source_target_pairs={{32,0},{17,1},{34,2},{19,3},{36,4},{21,5},{38,6},{23,7},{40,8},{25... | collective-permute-start | bytes 1544 | tf_op jit(solution)/shard_map/ppermute | solution.py:391
  96.8 4.6 %collective-permute-start.2 = (f32[1,128]{1,0:T(1,128)S(1)}, f32[1,128]{1,0:T(1,128)S(1)}, u32[]{:S(2)}, u32[]{:S(2)}) collective-permute-start(f32[1,128]{1,0:T(1,128)S(1)} %bitcast.29), channel_id=1, source_target_pairs={{0,64},{16,80},{32,96},{48,112},{64,0},{80,16},{96,32},{112,48},{1... | collective-permute-start | bytes 1544 | tf_op jit(solution)/shard_map/ppermute | solution.py:415
  101.3 6.0 %collective-permute-start.3 = (f32[1,128]{1,0:T(1,128)S(1)}, f32[1,128]{1,0:T(1,128)S(1)}, u32[]{:S(2)}, u32[]{:S(2)}) collective-permute-start(f32[1,128]{1,0:T(1,128)S(1)} %bitcast_add_fusion), channel_id=1, source_target_pairs={{0,128},{16,144},{32,160},{48,176},{64,192},{80,208},{96,224},{112... | collective-permute-start | bytes 1544 | tf_op jit(solution)/shard_map/ppermute | solution.py:415
  107.4 9.4 %collective-permute-start.4 = (f32[1,128]{1,0:T(1,128)S(1)}, f32[1,128]{1,0:T(1,128)S(1)}, u32[]{:S(2)}, u32[]{:S(2)}) collective-permute-start(f32[1,128]{1,0:T(1,128)S(1)} %add.31), channel_id=1, source_target_pairs={{0,256},{16,272},{32,288},{48,304},{64,320},{80,336},{96,352},{112... | collective-permute-start | bytes 1544 | tf_op jit(solution)/shard_map/ppermute | solution.py:415
  116.8 19.8 %collective-permute-start.5 = (f32[1,128]{1,0:T(1,128)S(1)}, f32[1,128]{1,0:T(1,128)S(1)}, u32[]{:S(2)}, u32[]{:S(2)}) collective-permute-start(f32[1,128]{1,0:T(1,128)S(1)} %get-tuple-element.40), channel_id=1, source_target_pairs={{8,0},{11,1},{10,2},{13,3},{12,4},{15,5},{14,6},{1,7},{0,8},{3,9},... | collective-permute-start | bytes 1544 | tf_op jit(solution)/shard_map/ppermute | solution.py:391
  121.9 14.6 %collective-permute-start.6 = (f32[1,128]{1,0:T(1,128)S(1)}, f32[1,128]{1,0:T(1,128)S(1)}, u32[]{:S(2)}, u32[]{:S(2)}) collective-permute-start(f32[1,128]{1,0:T(1,128)S(1)} %get-tuple-element.40), channel_id=1, source_target_pairs={{6,0},{13,1},{8,2},{15,3},{10,4},{1,5},{12,6},{3,7},{14,8},{5,9},{... | collective-permute-start | bytes 1544 | tf_op jit(solution)/shard_map/ppermute | solution.py:391
  125.9 10.6 %collective-permute-start.7 = (f32[1,128]{1,0:T(1,128)S(1)}, f32[1,128]{1,0:T(1,128)S(1)}, u32[]{:S(2)}, u32[]{:S(2)}) collective-permute-start(f32[1,128]{1,0:T(1,128)S(1)} %get-tuple-element.40), channel_id=1, source_target_pairs={{5,1},{7,3},{9,5},{11,7},{13,9},{15,11},{1,13},{3,15},{21,17},{23,... | collective-permute-start | bytes 1544 | tf_op jit(solution)/shard_map/ppermute | solution.py:391
  129.3 7.2 %collective-permute-start.8 = (f32[1,128]{1,0:T(1,128)S(1)}, f32[1,128]{1,0:T(1,128)S(1)}, u32[]{:S(2)}, u32[]{:S(2)}) collective-permute-start(f32[1,128]{1,0:T(1,128)S(1)} %get-tuple-element.40), channel_id=1, source_target_pairs={{2,0},{15,1},{4,2},{1,3},{6,4},{3,5},{8,6},{5,7},{10,8},{7,9},{12,... | collective-permute-start | bytes 1544 | tf_op jit(solution)/shard_map/ppermute | solution.py:391
  134.0 1.1 copy-start.9
  (1 other events, 0.8 us)

commit v4 on v3

--- a/solution.py
+++ b/solution.py
@@ -410,7 +410,7 @@
     sums = core_sum(sums)
     sums = core_sum(sum(ring_parts(sums, "dp", 1, 4)))
     clips = lax.axis_size("dp")
-    for stride in (4, 8, 16):
+    for stride in (16, 8, 4):
         if stride < clips:
             sums = sums + lax.ppermute(sums, "dp", [(i, i ^ stride) for i in range(clips)])
     parts = ring_parts(sums, "seq", 2, 8)

time: 140 us -> 140 us (level)
  no operation moved by 1% of the time
where the time goes in v4:
time: 140 us; the launch traced here: 139 us
  starting transfers between devices  55.5 us (40%)
  waiting for transfers between devices  52.6 us (38%)
  Pallas kernels  16.8 us (12%)
  local copies, waits for them, and re-layouts  7.55 us (5%)
  blocking collectives  5.81 us (4%)
    all_to_all x1, waiting for transfers between devices, local(): moved = exchange(packed)  47.7 us
    ppermute x6, starting transfers between devices, receive(): return lax.ppermute(sums, ('dp', 'seq'), pairs)  23.3 us
    ppermute x3, starting transfers between devices, local(): lax.ppermute(sums, 'dp', [(i, i ^ stride) for i in range(clips)])  16.1 us
    all_to_all x1, starting transfers between devices, local(): moved = exchange(packed)  10.5 us
    pallas_call x1, Pallas kernels, space(): pl.pallas_call(space_kernel, grid=(heads,), in_specs=[smem] * 3 + [block]...  9.02 us
    unnamed x28, local copies, waits for them, and re-layouts  6.97 us
    all_gather x3, blocking collectives, core_sum(): lax.all_gather(sums, 'seq', axis=0, tiled=True, axis_index_groups=cores)  5.81 us
    all_to_all x1, starting transfers between devices, local(): back = exchange(grads)  5.52 us
  transfers between devices with their start and end apart: 11, of which 6 were waited for; matrix products, arithmetic and copies ran while one was open for 0% of the time, Pallas kernels for 8%

profile of v4, /device:TPU:1, one launch (start us, length us, event | category | flops | bytes accessed | tf_op | source)
XLA Modules:
  0.0 139.2 jit_solution(7609874222147936339)
XLA Ops:
  0.6 3.0 %pack.1 = bf16[16,3,224,128]{3,2,1,0:T(8,128)(2,1)} custom-call(s32[32]{0:T(128)} %fc_hbm.3, s32[32]{0:T(128)} %pc_hbm.1, bf16[224,1536]{1,0:T(8,128)(2,1)} %bitcast.18, bf16[224,1536]{1,0:T(8,128)(2,1)} %bitcast.20, bf16[224,1536]{1,0:T(8,128)(2,1)} %bitcast.22, bf16[224,1536]{1,0:T(8,128)(2,1)} %bitcast.24), custom_call_target="tpu_custom_call" | custom-call | bytes 5505024 | tf_op jit(solution)/shard_map/pack/pallas_call | solution.py:107
  3.7 10.5 %all-to-all-start = ((bf16[16,3,224,128]{3,2,1,0:T(8,128)(2,1)}), bf16[16,3,224,128]{3,2,1,0:T(8,128)(2,1)S(1)}, u32[]{:S(2)}, u32[]{:S(2)}) async-start(bf16[16,3,224,128]{3,2,1,0:T(8,128)(2,1)} %pack.1), calls=%async_computation | async-start | bytes 5505024 | tf_op jit(solution)/shard_map/all_to_all | solution.py:406
  15.4 1.1 copy-done.2
  17.6 9.0 %space.1 = (bf16[224,1536]{1,0:T(8,128)(2,1)S(1)}, bf16[224,1536]{1,0:T(8,128)(2,1)S(1)}, bf16[224,1536]{1,0:T(8,128)(2,1)S(1)}, f32[1,128]{1,0:T(1,128)S(1)}) custom-call(s32[32]{0:T(128)S(1)} %copy-done.10, s32[32]{0:T(128)S(1)} %copy-done.11, f32[12]{0:T(128)S(1)} %copy-done.12, bf16[224,1536]{1,0:T(8,128)(2,1)S(1)} %bitcast.19, ...), custom_call_target="tpu_custom_call" | custom-call | flops 770703360 | bytes 6881280 | tf_op jit(solution)/shard_map/space/pallas_call | solution.py:167
  29.1 47.7 %all-to-all-done.moved_ref = bf16[16,3,224,128]{3,2,1,0:T(8,128)(2,1)S(1)} async-done(((bf16[16,3,224,128]{3,2,1,0:T(8,128)(2,1)}), bf16[16,3,224,128]{3,2,1,0:T(8,128)(2,1)S(1)}, u32[]{:S(2)}, u32[]{:S(2)}) %all-to-all-start) | async-done | bytes 2752544 | tf_op jit(solution)/shard_map/all_to_all | solution.py:406
  76.9 3.3 %time.1 = (bf16[16,3,168,128]{3,2,1,0:T(8,128)(2,1)}, f32[1,128]{1,0:T(1,128)S(1)}) custom-call(s32[32]{0:T(128)S(1)} %copy-done.10, f32[12]{0:T(128)S(1)} %copy-done.12, f32[12]{0:T(128)S(1)} %copy-done.13, f32[1,128]{1,0:T(1,128)S(1)} %get-tuple-element.22.space_sum_hbm, bf16[16,3,224,128]{3,2,1,0:T(8,128)(2,1)S(1)} %all-to-all-done.moved_ref), custom_call_target="tpu_custom_call" | custom-call | flops 440401920 | bytes 4816896 | tf_op jit(solution)/shard_map/time/pallas_call | solution.py:287
  80.2 5.5 %all-to-all-start.1 = ((bf16[16,3,168,128]{3,2,1,0:T(8,128)(2,1)}), bf16[16,3,168,128]{3,2,1,0:T(8,128)(2,1)S(1)}, u32[]{:S(2)}, u32[]{:S(2)}) async-start(bf16[16,3,168,128]{3,2,1,0:T(8,128)(2,1)} %get-tuple-element.23), calls=%async_computation.1 | async-start | bytes 4128768 | tf_op jit(solution)/shard_map/all_to_all | solution.py:409
  85.7 1.8 %all-gather = f32[2,1,128]{2,1,0:T(1,128)S(1)} all-gather(f32[1,1,128]{2,1,0:T(1,128)S(1)} %bitcast.26), channel_id=1, replica_groups={{0,1},{2,3},{4,5},{6,7},{8,9},{10,11},{12,13},{14,15},{16,17},{18,19},{..., dimensions={0}, use_global_device_ids=true | all-gather | bytes 1536 | tf_op jit(solution)/shard_map/all_gather | solution.py:367
  87.5 1.9 %collective-permute-start.1 = (f32[1,128]{1,0:T(1,128)S(1)}, f32[1,128]{1,0:T(1,128)S(1)}, u32[]{:S(2)}, u32[]{:S(2)}) collective-permute-start(f32[1,128]{1,0:T(1,128)S(1)} %bitcast.27), channel_id=1, source_target_pairs={{49,1},{51,3},{53,5},{55,7},{57,9},{59,11},{61,13},{63,15},{1,17},... | collective-permute-start | bytes 1544 | tf_op jit(solution)/shard_map/ppermute | solution.py:391
  89.4 4.6 %collective-permute-start = (f32[1,128]{1,0:T(1,128)S(1)}, f32[1,128]{1,0:T(1,128)S(1)}, u32[]{:S(2)}, u32[]{:S(2)}) collective-permute-start(f32[1,128]{1,0:T(1,128)S(1)} %bitcast.28), channel_id=1, source_target_pairs={{32,0},{17,1},{34,2},{19,3},{36,4},{21,5},{38,6},{23,7},{40,8},{25... | collective-permute-start | bytes 1544 | tf_op jit(solution)/shard_map/ppermute | solution.py:391
  94.7 2.1 %all-gather.1 = f32[2,1,128]{2,1,0:T(1,128)S(1)} all-gather(f32[1,1,128]{2,1,0:T(1,128)S(1)} %fusion.2), channel_id=1, replica_groups={{0,1},{2,3},{4,5},{6,7},{8,9},{10,11},{12,13},{14,15},{16,17},{18,19},{..., dimensions={0}, use_global_device_ids=true | all-gather | bytes 1536 | tf_op jit(solution)/shard_map/all_gather | solution.py:367
  96.8 9.0 %collective-permute-start.2 = (f32[1,128]{1,0:T(1,128)S(1)}, f32[1,128]{1,0:T(1,128)S(1)}, u32[]{:S(2)}, u32[]{:S(2)}) collective-permute-start(f32[1,128]{1,0:T(1,128)S(1)} %bitcast.29), channel_id=1, source_target_pairs={{0,256},{16,272},{32,288},{48,304},{64,320},{80,336},{96,352},{112... | collective-permute-start | bytes 1544 | tf_op jit(solution)/shard_map/ppermute | solution.py:415
  105.8 1.2 collective-permute-done.2
  107.0 4.0 %collective-permute-start.3 = (f32[1,128]{1,0:T(1,128)S(1)}, f32[1,128]{1,0:T(1,128)S(1)}, u32[]{:S(2)}, u32[]{:S(2)}) collective-permute-start(f32[1,128]{1,0:T(1,128)S(1)} %bitcast_add_fusion), channel_id=1, source_target_pairs={{0,128},{16,144},{32,160},{48,176},{64,192},{80,208},{96,224},{112... | collective-permute-start | bytes 1544 | tf_op jit(solution)/shard_map/ppermute | solution.py:415
  111.0 1.5 %collective-permute-done.3 = f32[1,128]{1,0:T(1,128)S(1)} collective-permute-done((f32[1,128]{1,0:T(1,128)S(1)}, f32[1,128]{1,0:T(1,128)S(1)}, u32[]{:S(2)}, u32[]{:S(2)}) %collective-permute-start.3) | collective-permute-done | bytes 544 | tf_op jit(solution)/shard_map/ppermute | solution.py:415
  112.5 3.1 %collective-permute-start.4 = (f32[1,128]{1,0:T(1,128)S(1)}, f32[1,128]{1,0:T(1,128)S(1)}, u32[]{:S(2)}, u32[]{:S(2)}) collective-permute-start(f32[1,128]{1,0:T(1,128)S(1)} %add.31), channel_id=1, source_target_pairs={{0,64},{16,80},{32,96},{48,112},{64,0},{80,16},{96,32},{112,48},{1... | collective-permute-start | bytes 1544 | tf_op jit(solution)/shard_map/ppermute | solution.py:415
  115.6 1.2 collective-permute-done.4
  116.8 5.1 %collective-permute-start.5 = (f32[1,128]{1,0:T(1,128)S(1)}, f32[1,128]{1,0:T(1,128)S(1)}, u32[]{:S(2)}, u32[]{:S(2)}) collective-permute-start(f32[1,128]{1,0:T(1,128)S(1)} %get-tuple-element.40), channel_id=1, source_target_pairs={{8,0},{11,1},{10,2},{13,3},{12,4},{15,5},{14,6},{1,7},{0,8},{3,9},... | collective-permute-start | bytes 1544 | tf_op jit(solution)/shard_map/ppermute | solution.py:391
  121.9 4.3 %collective-permute-start.6 = (f32[1,128]{1,0:T(1,128)S(1)}, f32[1,128]{1,0:T(1,128)S(1)}, u32[]{:S(2)}, u32[]{:S(2)}) collective-permute-start(f32[1,128]{1,0:T(1,128)S(1)} %get-tuple-element.40), channel_id=1, source_target_pairs={{6,0},{13,1},{8,2},{15,3},{10,4},{1,5},{12,6},{3,7},{14,8},{5,9},{... | collective-permute-start | bytes 1544 | tf_op jit(solution)/shard_map/ppermute | solution.py:391
  126.2 3.1 %collective-permute-start.7 = (f32[1,128]{1,0:T(1,128)S(1)}, f32[1,128]{1,0:T(1,128)S(1)}, u32[]{:S(2)}, u32[]{:S(2)}) collective-permute-start(f32[1,128]{1,0:T(1,128)S(1)} %get-tuple-element.40), channel_id=1, source_target_pairs={{5,1},{7,3},{9,5},{11,7},{13,9},{15,11},{1,13},{3,15},{21,17},{23,... | collective-permute-start | bytes 1544 | tf_op jit(solution)/shard_map/ppermute | solution.py:391
  129.3 4.3 %collective-permute-start.8 = (f32[1,128]{1,0:T(1,128)S(1)}, f32[1,128]{1,0:T(1,128)S(1)}, u32[]{:S(2)}, u32[]{:S(2)}) collective-permute-start(f32[1,128]{1,0:T(1,128)S(1)} %get-tuple-element.40), channel_id=1, source_target_pairs={{2,0},{15,1},{4,2},{1,3},{6,4},{3,5},{8,6},{5,7},{10,8},{7,9},{12,... | collective-permute-start | bytes 1544 | tf_op jit(solution)/shard_map/ppermute | solution.py:391
  134.0 1.1 copy-done.9
  135.1 1.4 %add.51 = (bf16[224,1536]{1,0:T(8,128)(2,1)}, bf16[224,1536]{1,0:T(8,128)(2,1)}, bf16[224,1536]{1,0:T(8,128)(2,1)}) custom-call(bf16[4,4,3,168,128]{4,3,2,1,0:T(8,128)(2,1)S(1)} %bitcast.17, bf16[224,1536]{1,0:T(8,128)(2,1)S(1)} %copy-done.5, bf16[224,1536]{1,0:T(8,128)(2,1)S(1)} %copy-done.7, bf16[224,1536]{1,0:T(8,128)(2,1)S(1)} %copy-done.9), custom_call_target="tpu_custom_call" | custom-call | flops 1032192 | bytes 6193152 | tf_op jit(solution)/shard_map/add/pallas_call | solution.py:348
  136.6 2.0 %all-gather.2 = f32[2,1,128]{2,1,0:T(1,128)S(1)} all-gather(f32[1,1,128]{2,1,0:T(1,128)S(1)} %add_bitcast_fusion), channel_id=1, replica_groups={{0,1},{2,3},{4,5},{6,7},{8,9},{10,11},{12,13},{14,15},{16,17},{18,19},{..., dimensions={0}, use_global_device_ids=true | all-gather | bytes 1536 | tf_op jit(solution)/shard_map/all_gather | solution.py:367
  (42 shorter events, 6.5 us)
Async XLA Ops:
  3.6 10.6 %copy-start = (bf16[1,1,224,1536]{3,2,1,0:T(8,128)(2,1)S(1)}, bf16[1,1,224,1536]{3,2,1,0:T(8,128)(2,1)}, u32[]{:S(2)}) copy-start(bf16[1,1,224,1536]{3,2,1,0:T(8,128)(2,1)} %param.8) | copy-start | bytes 2064388
  3.6 10.6 %copy-start.10 = (s32[32]{0:T(128)S(1)}, s32[32]{0:T(128)}, u32[]{:S(2)}) copy-start(s32[32]{0:T(128)} %fc_hbm.3) | copy-start | bytes 388
  3.7 10.6 %copy-start.11 = (s32[32]{0:T(128)S(1)}, s32[32]{0:T(128)}, u32[]{:S(2)}) copy-start(s32[32]{0:T(128)} %pc_hbm.1) | copy-start | bytes 388
  3.7 10.6 %copy-start.12 = (f32[12]{0:T(128)S(1)}, f32[12]{0:T(128)}, u32[]{:S(2)}) copy-start(f32[12]{0:T(128)} %scale_hbm.1) | copy-start | bytes 148
  3.7 73.2 %all-to-all-start = ((bf16[16,3,224,128]{3,2,1,0:T(8,128)(2,1)}), bf16[16,3,224,128]{3,2,1,0:T(8,128)(2,1)S(1)}, u32[]{:S(2)}, u32[]{:S(2)}) async-start(bf16[16,3,224,128]{3,2,1,0:T(8,128)(2,1)} %pack.1), calls=%async_computation | async-start | bytes 5505024 | tf_op jit(solution)/shard_map/all_to_all | solution.py:406
  14.3 1.1 copy-start.1
  15.4 1.1 copy-start.2
  16.5 1.1 copy-start.3
  17.6 59.3 %copy-start.13 = (f32[12]{0:T(128)S(1)}, f32[12]{0:T(128)}, u32[]{:S(2)}) copy-start(f32[12]{0:T(128)} %slope_hbm.1) | copy-start | bytes 148
  26.6 0.8 copy-start.4
  27.4 0.8 copy-start.6
  80.2 53.8 %copy-start.5 = (bf16[224,1536]{1,0:T(8,128)(2,1)S(1)}, bf16[224,1536]{1,0:T(8,128)(2,1)}, u32[]{:S(2)}) copy-start(bf16[224,1536]{1,0:T(8,128)(2,1)} %copy-done.4) | copy-start | bytes 2064388
  80.2 53.8 %copy-start.7 = (bf16[224,1536]{1,0:T(8,128)(2,1)S(1)}, bf16[224,1536]{1,0:T(8,128)(2,1)}, u32[]{:S(2)}) copy-start(bf16[224,1536]{1,0:T(8,128)(2,1)} %copy-done.6) | copy-start | bytes 2064388
  80.2 53.8 %all-to-all-start.1 = ((bf16[16,3,168,128]{3,2,1,0:T(8,128)(2,1)}), bf16[16,3,168,128]{3,2,1,0:T(8,128)(2,1)S(1)}, u32[]{:S(2)}, u32[]{:S(2)}) async-start(bf16[16,3,168,128]{3,2,1,0:T(8,128)(2,1)} %get-tuple-element.23), calls=%async_computation.1 | async-start | bytes 4128768 | tf_op jit(solution)/shard_map/all_to_all | solution.py:409
  87.5 6.5 %collective-permute-start.1 = (f32[1,128]{1,0:T(1,128)S(1)}, f32[1,128]{1,0:T(1,128)S(1)}, u32[]{:S(2)}, u32[]{:S(2)}) collective-permute-start(f32[1,128]{1,0:T(1,128)S(1)} %bitcast.27), channel_id=1, source_target_pairs={{49,1},{51,3},{53,5},{55,7},{57,9},{59,11},{61,13},{63,15},{1,17},... | collective-permute-start | bytes 1544 | tf_op jit(solution)/shard_map/ppermute | solution.py:391
  89.4 5.3 %collective-permute-start = (f32[1,128]{1,0:T(1,128)S(1)}, f32[1,128]{1,0:T(1,128)S(1)}, u32[]{:S(2)}, u32[]{:S(2)}) collective-permute-start(f32[1,128]{1,0:T(1,128)S(1)} %bitcast.28), channel_id=1, source_target_pairs={{32,0},{17,1},{34,2},{19,3},{36,4},{21,5},{38,6},{23,7},{40,8},{25... | collective-permute-start | bytes 1544 | tf_op jit(solution)/shard_map/ppermute | solution.py:391
  96.8 10.2 %collective-permute-start.2 = (f32[1,128]{1,0:T(1,128)S(1)}, f32[1,128]{1,0:T(1,128)S(1)}, u32[]{:S(2)}, u32[]{:S(2)}) collective-permute-start(f32[1,128]{1,0:T(1,128)S(1)} %bitcast.29), channel_id=1, source_target_pairs={{0,256},{16,272},{32,288},{48,304},{64,320},{80,336},{96,352},{112... | collective-permute-start | bytes 1544 | tf_op jit(solution)/shard_map/ppermute | solution.py:415
  107.0 5.5 %collective-permute-start.3 = (f32[1,128]{1,0:T(1,128)S(1)}, f32[1,128]{1,0:T(1,128)S(1)}, u32[]{:S(2)}, u32[]{:S(2)}) collective-permute-start(f32[1,128]{1,0:T(1,128)S(1)} %bitcast_add_fusion), channel_id=1, source_target_pairs={{0,128},{16,144},{32,160},{48,176},{64,192},{80,208},{96,224},{112... | collective-permute-start | bytes 1544 | tf_op jit(solution)/shard_map/ppermute | solution.py:415
  112.5 4.3 %collective-permute-start.4 = (f32[1,128]{1,0:T(1,128)S(1)}, f32[1,128]{1,0:T(1,128)S(1)}, u32[]{:S(2)}, u32[]{:S(2)}) collective-permute-start(f32[1,128]{1,0:T(1,128)S(1)} %add.31), channel_id=1, source_target_pairs={{0,64},{16,80},{32,96},{48,112},{64,0},{80,16},{96,32},{112,48},{1... | collective-permute-start | bytes 1544 | tf_op jit(solution)/shard_map/ppermute | solution.py:415
  116.8 19.8 %collective-permute-start.5 = (f32[1,128]{1,0:T(1,128)S(1)}, f32[1,128]{1,0:T(1,128)S(1)}, u32[]{:S(2)}, u32[]{:S(2)}) collective-permute-start(f32[1,128]{1,0:T(1,128)S(1)} %get-tuple-element.40), channel_id=1, source_target_pairs={{8,0},{11,1},{10,2},{13,3},{12,4},{15,5},{14,6},{1,7},{0,8},{3,9},... | collective-permute-start | bytes 1544 | tf_op jit(solution)/shard_map/ppermute | solution.py:391
  121.9 14.6 %collective-permute-start.6 = (f32[1,128]{1,0:T(1,128)S(1)}, f32[1,128]{1,0:T(1,128)S(1)}, u32[]{:S(2)}, u32[]{:S(2)}) collective-permute-start(f32[1,128]{1,0:T(1,128)S(1)} %get-tuple-element.40), channel_id=1, source_target_pairs={{6,0},{13,1},{8,2},{15,3},{10,4},{1,5},{12,6},{3,7},{14,8},{5,9},{... | collective-permute-start | bytes 1544 | tf_op jit(solution)/shard_map/ppermute | solution.py:391
  126.2 10.3 %collective-permute-start.7 = (f32[1,128]{1,0:T(1,128)S(1)}, f32[1,128]{1,0:T(1,128)S(1)}, u32[]{:S(2)}, u32[]{:S(2)}) collective-permute-start(f32[1,128]{1,0:T(1,128)S(1)} %get-tuple-element.40), channel_id=1, source_target_pairs={{5,1},{7,3},{9,5},{11,7},{13,9},{15,11},{1,13},{3,15},{21,17},{23,... | collective-permute-start | bytes 1544 | tf_op jit(solution)/shard_map/ppermute | solution.py:391
  129.3 7.2 %collective-permute-start.8 = (f32[1,128]{1,0:T(1,128)S(1)}, f32[1,128]{1,0:T(1,128)S(1)}, u32[]{:S(2)}, u32[]{:S(2)}) collective-permute-start(f32[1,128]{1,0:T(1,128)S(1)} %get-tuple-element.40), channel_id=1, source_target_pairs={{2,0},{15,1},{4,2},{1,3},{6,4},{3,5},{8,6},{5,7},{10,8},{7,9},{12,... | collective-permute-start | bytes 1544 | tf_op jit(solution)/shard_map/ppermute | solution.py:391
  134.0 1.1 copy-start.9
  (1 other events, 0.8 us)
